TPU v7x, 32 devices: a whole 2x2x4 slice. The times are simulated.
32 devices in a mesh: dp: 16 (over z, y, x), pair: 2 (over core).
Axes of the slice: x: 2, y: 2, z: 4, core: 2. Of those that a mesh axis runs over, the one named last changes fastest.
Arguments:
- hidden: bfloat16 [16384, 1024], P('dp'), may hold values from -6 to 6
- doc_lengths: int32 [16, 8], P('dp'), may hold values from 1 to 512, 1024 in all within a row
- ln_gain: float32 [1024], replicated, may hold values from 0.5 to 1.5
- ln_bias: float32 [1024], replicated, may hold values from -3 to 3
- qkv_weight: bfloat16 [1024, 3072], replicated, may hold values from -0.1875 to 0.1875
- qkv_bias: float32 [3072], replicated, may hold values from -3 to 3
- dense_weight: bfloat16 [1024, 1024], replicated, may hold values from -1.5 to 1.5
- dense_bias: float32 [1024], replicated, may hold values from -2 to 2
- fc_in_weight: bfloat16 [1024, 4096], replicated, may hold values from -0.1875 to 0.1875
- fc_in_bias: float32 [4096], replicated, may hold values from -3 to 3
- fc_out_weight: bfloat16 [4096, 1024], replicated, may hold values from -0.09375 to 0.09375
- fc_out_bias: float32 [1024], replicated, may hold values from -2 to 2
- cotangent: bfloat16 [16384, 1024], P('dp'), may hold values from -6 to 6
Outputs:
- output: bfloat16 [16384, 1024], P(('dp', 'pair'))
- input_grad: bfloat16 [16384, 1024], P('dp')
- qkv_weight_grad: float32 [1024, 3072], P(('dp', 'pair'))
- qkv_bias_grad: float32 [3072], P(('dp', 'pair'))
- dense_weight_grad: float32 [1024, 1024], P(('dp', 'pair'))
- dense_bias_grad: float32 [1024], P(('dp', 'pair'))
- fc_in_weight_grad: float32 [1024, 4096], P(('dp', 'pair'))
- fc_in_bias_grad: float32 [4096], P(('dp', 'pair'))
- fc_out_weight_grad: float32 [4096, 1024], P(('dp', 'pair'))
- fc_out_bias_grad: float32 [1024], P(('dp', 'pair'))
- ln_gain_grad: float32 [1024], P(('dp', 'pair'))
- ln_bias_grad: float32 [1024], P(('dp', 'pair'))
Inputs may be any that keep to these rules, and one draw needn't show every extreme that they name: `doc_lengths`: each row holds the lengths of the 8 documents packed into one sequence, in order; they sum to 1024, and in every row one document has 512 tokens.
All inputs are finite; a program needn't handle non-finite values.
Results may differ from a plain program's by a relative error of at most 0.011.
Values may be sent and summed in bfloat16 or wider, within the bound.
A program may use at most 448 MiB of HBM per device.

v0:
```python
from functools import partial

import jax
import jax.numpy as jnp
from jax import lax
from jax.sharding import PartitionSpec as P

HEADS = 16
HEAD = 64
ROT = 16
SEQ_LEN = 1024
DOCS = 8


norm_epsilon = 1e-05


def partner_2(array, axis, apart):
    return lax.ppermute(array, axis, [(i, i ^ 1 << apart) for i in range(lax.axis_size(axis))])


def token_tables(doc_lengths):
    doc_ends = jnp.cumsum(doc_lengths, axis=1)
    doc_starts = doc_ends - doc_lengths
    places = jnp.arange(SEQ_LEN, dtype=jnp.int32)
    doc_of = jnp.sum((places[None, :, None] >= doc_ends[:, None, :]).astype(jnp.int32), axis=2)
    picked = doc_of[:, :, None] == jnp.arange(DOCS, dtype=jnp.int32)[None, None, :]
    start_of = jnp.sum(jnp.where(picked, doc_starts[:, None, :], 0), axis=2)
    positions = places[None, :] - start_of
    inverse = 10000.0 ** (-(jnp.arange(0, ROT, 2, dtype=jnp.float32) / ROT))
    angles = positions.astype(jnp.float32)[:, :, None] * inverse[None, None, :]
    cosines = jnp.concatenate([jnp.cos(angles), jnp.cos(angles)], axis=2).reshape(-1, ROT)
    sines = jnp.concatenate([jnp.sin(angles), jnp.sin(angles)], axis=2).reshape(-1, ROT)
    places_all = places[None, :].reshape(-1)
    return (doc_of.reshape(-1), places_all, cosines, sines)


def rotate(values, cosines, sines):
    half_rot = ROT // 2
    turned_part = values[..., :ROT]
    swapped = jnp.concatenate([-turned_part[..., half_rot:], turned_part[..., :half_rot]], axis=-1)
    turned = turned_part * cosines[:, None, :] + swapped * sines[:, None, :]
    return jnp.concatenate([turned, values[..., ROT:]], axis=-1)


def rotate_back(grads, cosines, sines):
    half_rot = ROT // 2
    turned_part = grads[..., :ROT]
    scaled = turned_part * sines[:, None, :]
    swapped = jnp.concatenate([scaled[..., half_rot:], -scaled[..., :half_rot]], axis=-1)
    return jnp.concatenate([turned_part * cosines[:, None, :] + swapped, grads[..., ROT:]], axis=-1)


def block_mask(doc_ids, places, first_row, row_count):
    query_docs = lax.dynamic_slice_in_dim(doc_ids, first_row, row_count, 0)
    query_places = lax.dynamic_slice_in_dim(places, first_row, row_count, 0)
    return (query_docs[:, None] == doc_ids[None, :]) & (places[None, :] <= query_places[:, None])


def block_scores(queries, keys_all, doc_ids, places, index, row_count):
    first_row = index * row_count
    seq_start = first_row // SEQ_LEN * SEQ_LEN
    query_block = lax.dynamic_slice_in_dim(queries, first_row, row_count, 0)
    allowed = block_mask(doc_ids, places, first_row, row_count)
    scores = jnp.einsum(
        "qhd,khd->hqk", query_block, keys_all, preferred_element_type=jnp.float32
    ) * HEAD ** (-0.5)
    return (
        jnp.where(allowed[None], scores, -1000000000.0),
        query_block,
        keys_all,
        first_row,
        seq_start,
    )


def attend(queries, keys_all, values_all, doc_ids, places, row_count):
    block_count = queries.shape[0] // row_count

    def one_block(index):
        scores, query_block, key_seq, first_row, seq_start = block_scores(
            queries, keys_all, doc_ids, places, index, row_count
        )
        top_score = jnp.max(scores, axis=2, keepdims=True)
        shifted = jnp.exp(scores - top_score)
        totals = jnp.sum(shifted, axis=2, keepdims=True)
        probs_b = (shifted / totals).astype(jnp.bfloat16)
        context = jnp.einsum(
            "hqk,khd->qhd", probs_b, values_all, preferred_element_type=jnp.float32
        )
        return (context, (top_score + jnp.log(totals))[:, :, 0])

    context, log_totals = lax.map(one_block, jnp.arange(block_count, dtype=jnp.int32))
    return (context.reshape(queries.shape), log_totals)


def attend_back(queries, keys_all, values_all, d_context, log_totals, doc_ids, places, row_count):
    block_count = queries.shape[0] // row_count

    def one_block(sums, index):
        key_sum, value_sum = sums
        scores, query_block, key_seq, first_row, seq_start = block_scores(
            queries, keys_all, doc_ids, places, index, row_count
        )
        grad_block = lax.dynamic_slice_in_dim(d_context, first_row, row_count, 0)
        probs = jnp.exp(scores - log_totals[index][:, :, None])
        d_probs = jnp.einsum(
            "qhd,khd->hqk", grad_block, values_all, preferred_element_type=jnp.float32
        )
        inner = jnp.sum(probs * d_probs, axis=2, keepdims=True)
        d_scores = (probs * (d_probs - inner)).astype(jnp.bfloat16)
        d_query = jnp.einsum(
            "hqk,khd->qhd", d_scores, key_seq, preferred_element_type=jnp.float32
        ) * HEAD ** (-0.5)
        d_key = jnp.einsum(
            "hqk,qhd->khd", d_scores, query_block, preferred_element_type=jnp.float32
        ) * HEAD ** (-0.5)
        d_value = jnp.einsum(
            "hqk,qhd->khd",
            probs.astype(jnp.bfloat16),
            grad_block,
            preferred_element_type=jnp.float32,
        )
        key_sum = key_sum + d_key
        value_sum = value_sum + d_value
        return ((key_sum, value_sum), d_query)

    empty = jnp.zeros(queries.shape, jnp.float32)
    (key_sum, value_sum), d_query = lax.scan(
        one_block, (empty, empty), jnp.arange(block_count, dtype=jnp.int32)
    )
    return (d_query.reshape(queries.shape), key_sum, value_sum)


def body(
    hidden,
    doc_lengths,
    ln_gain,
    ln_bias,
    qkv_weight,
    qkv_bias,
    dense_weight,
    dense_bias,
    fc_in_weight,
    fc_in_bias,
    fc_out_weight,
    fc_out_bias,
    cotangent,
):
    token_count = hidden.shape[0]
    width = hidden.shape[1]
    hidden_units = fc_in_weight.shape[1]
    row_count = min(512, SEQ_LEN)
    block_count = token_count // row_count
    head_shape = (token_count, HEADS, HEAD)
    pair_index = lax.axis_index("pair")
    on_attention = pair_index == 0
    half_rows = token_count // 2
    first_half = pair_index * half_rows
    other_half = (1 - pair_index) * half_rows
    inputs = hidden.astype(jnp.float32)
    row_mean = jnp.mean(inputs, axis=1, keepdims=True)
    centred = inputs - row_mean
    inv_std = lax.rsqrt(jnp.mean(centred * centred, axis=1, keepdims=True) + norm_epsilon)
    x_hat = centred * inv_std
    normed = (x_hat * ln_gain + ln_bias).astype(jnp.bfloat16)
    doc_ids, places, cosines, sines = token_tables(doc_lengths)

    def attention_forward(normed_in):
        raw = jnp.dot(normed_in, qkv_weight, preferred_element_type=jnp.float32) + qkv_bias
        queries = rotate(raw[:, :width].reshape(head_shape), cosines, sines).astype(jnp.bfloat16)
        keys_b = rotate(raw[:, width : 2 * width].reshape(head_shape), cosines, sines).astype(
            jnp.bfloat16
        )
        values_b = raw[:, 2 * width :].reshape(head_shape).astype(jnp.bfloat16)
        context, log_totals = attend(queries, keys_b, values_b, doc_ids, places, row_count)
        context_b = context.reshape(token_count, width).astype(jnp.bfloat16)
        branch = (
            jnp.dot(context_b, dense_weight, preferred_element_type=jnp.float32) + dense_bias
        ).astype(jnp.bfloat16)
        kept = jnp.concatenate(
            [
                queries.reshape(token_count, width),
                keys_b.reshape(token_count, width),
                values_b.reshape(token_count, width),
            ],
            axis=1,
        )
        return (
            branch,
            kept,
            context_b,
            log_totals,
            jnp.zeros((token_count, hidden_units), jnp.float32),
        )

    def feed_forward(normed_in):
        pre_act = jnp.dot(normed_in, fc_in_weight, preferred_element_type=jnp.float32) + fc_in_bias
        act_b = jax.nn.gelu(pre_act, approximate=False).astype(jnp.bfloat16)
        branch = (
            jnp.dot(act_b, fc_out_weight, preferred_element_type=jnp.float32) + fc_out_bias
        ).astype(jnp.bfloat16)
        return (
            branch,
            jnp.zeros((token_count, 3 * width), jnp.bfloat16),
            jnp.zeros((token_count, width), jnp.bfloat16),
            jnp.zeros((block_count, HEADS, row_count), jnp.float32),
            pre_act,
        )

    branch, kept_qkv, context_b, log_totals, pre_act = lax.cond(
        on_attention, attention_forward, feed_forward, normed
    )
    sent_rows = lax.dynamic_slice_in_dim(branch, other_half, half_rows, 0)
    own_rows = lax.dynamic_slice_in_dim(branch, first_half, half_rows, 0)
    partner = partner_2(sent_rows, "pair", 0)
    attn_part = jnp.where(on_attention, own_rows, partner).astype(jnp.float32)
    mlp_part = jnp.where(on_attention, partner, own_rows).astype(jnp.float32)
    input_rows = lax.dynamic_slice_in_dim(inputs, first_half, half_rows, 0)
    output = (input_rows + attn_part + mlp_part).astype(jnp.bfloat16)
    grad_out = cotangent.astype(jnp.float32)

    def attention_top(grad_in):
        dense_w_grad = jnp.einsum(
            "td,te->de", context_b, cotangent, preferred_element_type=jnp.float32
        )
        dense_b_grad = jnp.sum(grad_in, axis=0)
        d_context = jnp.einsum(
            "te,de->td", cotangent, dense_weight, preferred_element_type=jnp.float32
        ).astype(jnp.bfloat16)
        return (
            (
                dense_w_grad,
                dense_b_grad,
                jnp.zeros((hidden_units, width), jnp.float32),
                jnp.zeros((width,), jnp.float32),
            ),
            d_context,
            jnp.zeros((token_count, hidden_units), jnp.float32),
        )

    def feed_top(grad_in):
        act_b = jax.nn.gelu(pre_act, approximate=False).astype(jnp.bfloat16)
        out_w_grad = jnp.einsum("tf,te->fe", act_b, cotangent, preferred_element_type=jnp.float32)
        out_b_grad = jnp.sum(grad_in, axis=0)
        d_act = jnp.einsum(
            "te,fe->tf", cotangent, fc_out_weight, preferred_element_type=jnp.float32
        )
        return (
            (
                jnp.zeros((width, width), jnp.float32),
                jnp.zeros((width,), jnp.float32),
                out_w_grad,
                out_b_grad,
            ),
            jnp.zeros((token_count, width), jnp.bfloat16),
            d_act,
        )

    top_grads, d_context, d_act = lax.cond(on_attention, attention_top, feed_top, grad_out)

    def attention_rest(d_context_in):
        queries = kept_qkv[:, :width].reshape(head_shape)
        keys_b = kept_qkv[:, width : 2 * width].reshape(head_shape)
        values_b = kept_qkv[:, 2 * width :].reshape(head_shape)
        d_query, d_key, d_value = attend_back(
            queries,
            keys_b,
            values_b,
            d_context_in.reshape(head_shape),
            log_totals,
            doc_ids,
            places,
            row_count,
        )
        d_raw = jnp.concatenate(
            [
                rotate_back(d_query, cosines, sines).reshape(token_count, width),
                rotate_back(d_key, cosines, sines).reshape(token_count, width),
                d_value.reshape(token_count, width),
            ],
            axis=1,
        ).astype(jnp.bfloat16)
        qkv_w_grad = jnp.einsum("td,tc->dc", normed, d_raw, preferred_element_type=jnp.float32)
        qkv_b_grad = jnp.sum(d_raw, axis=0, dtype=jnp.float32)
        d_normed_part = jnp.einsum(
            "tc,dc->td", d_raw, qkv_weight, preferred_element_type=jnp.float32
        )
        return (
            d_normed_part,
            (
                qkv_w_grad,
                qkv_b_grad,
                jnp.zeros((width, hidden_units), jnp.float32),
                jnp.zeros((hidden_units,), jnp.float32),
            ),
        )

    def feed_rest(d_context_in):
        slope = jax.vjp(partial(jax.nn.gelu, approximate=False), pre_act)[1](d_act)[0]
        d_pre = slope.astype(jnp.bfloat16)
        in_w_grad = jnp.einsum("td,tf->df", normed, d_pre, preferred_element_type=jnp.float32)
        in_b_grad = jnp.sum(d_pre, axis=0, dtype=jnp.float32)
        d_normed_part = jnp.einsum(
            "tf,df->td", d_pre, fc_in_weight, preferred_element_type=jnp.float32
        )
        return (
            d_normed_part,
            (
                jnp.zeros((width, 3 * width), jnp.float32),
                jnp.zeros((3 * width,), jnp.float32),
                in_w_grad,
                in_b_grad,
            ),
        )

    d_normed_own, rest_grads = lax.cond(on_attention, attention_rest, feed_rest, d_context)
    d_normed_other = partner_2(d_normed_own.astype(jnp.bfloat16), "pair", 0).astype(
        d_normed_own.dtype
    )
    d_normed = (d_normed_own + d_normed_other).astype(jnp.bfloat16).astype(jnp.float32)
    scaled = d_normed * ln_gain
    input_grad = (
        grad_out
        + inv_std
        * (
            scaled
            - jnp.mean(scaled, axis=1, keepdims=True)
            - x_hat * jnp.mean(scaled * x_hat, axis=1, keepdims=True)
        )
    ).astype(jnp.bfloat16)
    half_grads = lax.dynamic_slice_in_dim(d_normed, first_half, half_rows, 0)
    half_hat = lax.dynamic_slice_in_dim(x_hat, first_half, half_rows, 0)
    gain_grad = jnp.sum(half_grads * half_hat, axis=0)
    bias_grad = jnp.sum(half_grads, axis=0)
    summed = (
        lax.psum_scatter(rest_grads[0], ("dp", "pair"), scatter_dimension=0, tiled=True),
        lax.psum_scatter(rest_grads[1], ("dp", "pair"), scatter_dimension=0, tiled=True),
        lax.psum_scatter(top_grads[0], ("dp", "pair"), scatter_dimension=0, tiled=True),
        lax.psum_scatter(top_grads[1], ("dp", "pair"), scatter_dimension=0, tiled=True),
        lax.psum_scatter(rest_grads[2], ("dp", "pair"), scatter_dimension=0, tiled=True),
        lax.psum_scatter(rest_grads[3], ("dp", "pair"), scatter_dimension=0, tiled=True),
        lax.psum_scatter(top_grads[2], ("dp", "pair"), scatter_dimension=0, tiled=True),
        lax.psum_scatter(top_grads[3], ("dp", "pair"), scatter_dimension=0, tiled=True),
        lax.psum_scatter(gain_grad, ("dp", "pair"), scatter_dimension=0, tiled=True),
        lax.psum_scatter(bias_grad, ("dp", "pair"), scatter_dimension=0, tiled=True),
    )
    (
        qkv_w_sum,
        qkv_b_sum,
        dense_w_sum,
        dense_b_sum,
        in_w_sum,
        in_b_sum,
        out_w_sum,
        out_b_sum,
        gain_sum,
        bias_sum,
    ) = summed
    return (
        output,
        input_grad,
        qkv_w_sum,
        qkv_b_sum,
        dense_w_sum,
        dense_b_sum,
        in_w_sum,
        in_b_sum,
        out_w_sum,
        out_b_sum,
        gain_sum,
        bias_sum,
    )


def solution(mesh):
    return jax.shard_map(
        body,
        mesh=mesh,
        in_specs=(
            P("dp", None),
            P("dp", None),
            P(),
            P(),
            P(),
            P(),
            P(),
            P(),
            P(),
            P(),
            P(),
            P(),
            P("dp", None),
        ),
        out_specs=(
            P(("dp", "pair"), None),
            P("dp", None),
            P(("dp", "pair"), None),
            P(("dp", "pair")),
            P(("dp", "pair"), None),
            P(("dp", "pair")),
            P(("dp", "pair"), None),
            P(("dp", "pair")),
            P(("dp", "pair"), None),
            P(("dp", "pair")),
            P(("dp", "pair")),
            P(("dp", "pair")),
        ),
        check_vma=False,
    )
```

profile of v0, /device:TPU:3, one launch (start us, length us, event | category | flops | bytes accessed | tf_op | source)
XLA Modules:
  0.0 1181.4 jit_solution(8897148399874951065)
XLA Ops:
  13.4 4.6 convert_element_type.133
  18.2 5.7 subtract_multiply_fusion
  24.6 74.5 %conditional.16 = (bf16[1024,3072]{1,0:T(8,128)(2,1)}, bf16[1024,1024]{1,0:T(8,128)(2,1)}, f32[2,16,512]{2,1,0:T(8,128)}, f32[1024,4096]{1,0:T(8,128)}, bf16[1024,1024]{1,0:T(8,128)(2,1)}) conditional(s32[]{:T(128)} %convert_element_type.126, (bf16[1024,1024]{1,0:T(8,128)(2,1)}, bf16[1024,4096]{1,0:T(8,128)(2,1)}, f32[4096]{0:T(1024)S(1)}, ...), branch_computations={%region_5.6_spmd, %region_6.11_spmd} | conditional | flops 17458790400 | bytes 279401024
  24.8 16.1 %broadcast_add_fusion = f32[1024,4096]{1,0:T(8,128)} fusion(f32[4096]{0:T(1024)S(1)} %get-tuple-element.303, bf16[1024,1024]{1,0:T(8,128)(2,1)} %get-tuple-element.186, bf16[1024,4096]{1,0:T(8,128)(2,1)} %get-tuple-element.187), kind=kOutput, calls=%fused_computation.19 | convolution fusion | flops 8594128896 | bytes 27279360 | tf_op jit(solution)/shard_map/cond/branch_0_fun/dot_general | solution.py:198
  40.8 45.6 %fusion.12 = bf16[1024,1024]{1,0:T(8,128)(2,1)} fusion(bf16[4096,1024]{1,0:T(8,128)(2,1)S(1)} %get-tuple-element.189, f32[1024,4096]{1,0:T(8,128)} %broadcast_add_fusion, f32[1024]{0:T(1024)S(1)} %get-tuple-element.304), kind=kOutput, calls=%fused_computation.21 | convolution fusion | flops 8864661504 | bytes 27267072 | tf_op jit(solution)/shard_map/cond/branch_0_fun/dot_general | solution.py:201
  86.4 3.5 broadcast.509
  99.1 68.3 %conditional.6 = (f32[1024,1024]{1,0:T(8,128)}, f32[1024]{0:T(1024)S(1)}, f32[4096,1024]{1,0:T(8,128)}, f32[1024]{0:T(1024)S(1)}, bf16[1024,1024]{1,0:T(8,128)(2,1)}, /*index=5*/f32[1024,4096]{1,0:T(8,128)}) conditional(s32[]{:T(128)} %convert_element_type.126, (f32[1024,4096]{1,0:T(8,128)}, bf16[1024,1024]{1,0:T(8,128)(2,1)}, ...), branch_computations={%region_11.13_spmd, %region_13.15_spmd} | conditional | flops 17453547520 | bytes 81797216 | solution.py:260
  99.1 46.6 %fusion.65 = f32[4096,1024]{1,0:T(8,128)} fusion(bf16[1024,1024]{1,0:T(8,128)(2,1)} %get-tuple-element.217, f32[1024,4096]{1,0:T(8,128)} %get-tuple-element.216), kind=kOutput, calls=%fused_computation.99 | convolution fusion | flops 8862564352 | bytes 35651584 | tf_op jit(solution)/shard_map/cond/branch_0_fun/tf,te->fe/dot_general | solution.py:244
  148.2 14.6 %fusion.136 = f32[1024,4096]{1,0:T(8,128)} fusion(bf16[1024,1024]{1,0:T(8,128)(2,1)S(1)} %copy-done.2, bf16[4096,1024]{1,0:T(8,128)(2,1)} %get-tuple-element.219), kind=kOutput, calls=%fused_computation.225 | convolution fusion | flops 8589934592 | bytes 27262976 | tf_op jit(solution)/shard_map/cond/branch_0_fun/te,fe->tf/dot_general | solution.py:246
  168.0 87.6 %conditional.7 = (f32[1024,1024]{1,0:T(8,128)}, f32[1024,3072]{1,0:T(8,128)}, f32[3072]{0:T(1024)}, f32[1024,4096]{0,1:T(8,128)}, f32[4096]{0:T(1024)}) conditional(s32[]{:T(128)} %convert_element_type.126, (f32[1024,4096]{1,0:T(8,128)}, f32[1024,4096]{1,0:T(8,128)}, bf16[1024,4096]{1,0:T(8,128)(2,1)}, bf16[1024,1024]{1,0:T(8,128)(2,1)}) %tuple.54, ...), branch_computations={%region_15.17_spmd, %region_17.22_spmd} | conditional | flops 18458857472 | bytes 473875136 | solution.py:317
  176.6 43.1 %convert_reduce_fusion = (f32[4096]{0:T(1024)}, bf16[1024,4096]{1,0:T(8,128)(2,1)S(1)}) fusion(f32[1024,4096]{1,0:T(8,128)} %get-tuple-element.225, f32[1024,4096]{1,0:T(8,128)} %get-tuple-element.224), kind=kLoop, calls=%fused_computation.137 | loop fusion | flops 310374400 | bytes 41959424 | tf_op jit(solution)/shard_map/cond/branch_0_fun/reduce_sum | solution.py:303
  219.7 10.4 fusion.138
  230.1 13.7 %convolution_bitcast_fusion = f32[1024,4096]{0,1:T(8,128)} fusion(bf16[1024,4096]{1,0:T(8,128)(2,1)S(1)} %get-tuple-element.511, bf16[1024,1024]{1,0:T(8,128)(2,1)} %get-tuple-element.227), kind=kOutput, calls=%fused_computation.153 | convolution fusion | flops 8589934592 | bytes 27262976 | tf_op jit(solution)/shard_map/cond/branch_0_fun/td,tf->df/dot_general | solution.py:302
  243.8 6.0 broadcast.613
  255.7 17.5 %copy.80 = f32[1024,4096]{1,0:T(8,128)} copy(f32[1024,4096]{0,1:T(8,128)} %get-tuple-element.297) | data formatting | bytes 33554432 | tf_op jit(solution)/shard_map/cond | solution.py:317
  273.9 4.0 convert_element_type.134
  277.9 389.4 %collective-permute-start.1 = (bf16[1024,1024]{1,0:T(8,128)(2,1)}, bf16[1024,1024]{1,0:T(8,128)(2,1)}, u32[]{:S(2)}, u32[]{:S(2)}) collective-permute-start(bf16[1024,1024]{1,0:T(8,128)(2,1)} %convert_element_type.134), channel_id=1, source_target_pairs={{0,1},{1,0},{2,3},{3,2},{4,5},{5,4},{6,7},{7,6},{8,9},{9,8},{10,11... | collective-permute-start | bytes 6291464 | tf_op jit(solution)/shard_map/ppermute | solution.py:19
  673.3 3.9 add_convert_fusion.3
  677.2 5.4 fusion.131
  683.1 42.2 %all-reduce.6 = (f32[3072]{0:T(1024)S(1)}, f32[1024]{0:T(1024)S(1)}, f32[4096]{0:T(1024)S(1)}, f32[1024]{0:T(1024)S(1)}, f32[1024]{0:T(1024)S(1)}, /*index=5*/f32[1024]{0:T(1024)S(1)}) all-reduce(f32[3072]{0:T(1024)} %get-tuple-element.294, f32[1024]{0:T(1024)S(1)} %copy-done.27, ...), channel_id=3, replica_groups=mesh['dp'=16,'pair'=2] {'dp','pair'}, use_global_device_ids=true, to_apply=%region_25.26.clone | all-reduce | flops 11264 | bytes 90112
  731.8 4.4 add_convert_fusion
  736.2 65.5 %reduce-scatter.5.cloned.1.call-done = f32[32,3072]{1,0:T(8,128)} async-done(((f32[1024,3072]{1,0:T(8,128)}), f32[32,3072]{1,0:T(8,128)}) %reduce-scatter.5.cloned.1.call-update) | async-done | bytes 393232 | tf_op jit(solution)/shard_map/reduce_scatter | solution.py:337
  801.7 185.6 %reduce-scatter.9.cloned.1.call-done = f32[32,4096]{1,0:T(8,128)} async-done(((f32[1024,4096]{1,0:T(8,128)}), f32[32,4096]{1,0:T(8,128)}) %reduce-scatter.9.cloned.1.call-update) | async-done | bytes 524304 | tf_op jit(solution)/shard_map/reduce_scatter | solution.py:341
  987.3 187.3 %reduce-scatter.11.cloned.1.call-done = f32[128,1024]{1,0:T(8,128)} async-done(((f32[4096,1024]{1,0:T(8,128)}), f32[128,1024]{1,0:T(8,128)}) %reduce-scatter.11.cloned.1.call-update) | async-done | bytes 524304 | tf_op jit(solution)/shard_map/reduce_scatter | solution.py:343
  (87 shorter events, 30.5 us)
Async XLA Ops:
  7.2 17.3 %copy-start.31 = (f32[4096]{0:T(1024)S(1)}, f32[4096]{0:T(1024)}, u32[]{:S(2)}) copy-start(f32[4096]{0:T(1024)} %param.32) | copy-start | bytes 49156
  7.2 17.3 %copy-start.33 = (f32[1024]{0:T(1024)S(1)}, f32[1024]{0:T(1024)}, u32[]{:S(2)}) copy-start(f32[1024]{0:T(1024)} %param.34) | copy-start | bytes 12292
  7.2 17.3 %copy-start.32 = (f32[3072]{0:T(1024)S(1)}, f32[3072]{0:T(1024)}, u32[]{:S(2)}) copy-start(f32[3072]{0:T(1024)} %param.28) | copy-start | bytes 36868
  7.2 729.0 %reduce-scatter.7.cloned.1.call-start = ((), (), s32[]{:S(2)}) async-start(), calls=%async_computation.5 | async-start | bytes 4325376 | tf_op jit(solution)/shard_map/reduce_scatter | solution.py:339
  9.2 15.3 %copy-start.19 = (f32[1024]{0:T(1024)}, f32[1024]{0:T(1024)S(1)}, u32[]{:S(2)}) copy-start(f32[1024]{0:T(1024)S(1)} %broadcast_multiply_fusion.2) | copy-start | bytes 12292
  11.5 13.0 %copy-start.21 = (f32[1024]{0:T(1024)}, f32[1024]{0:T(1024)S(1)}, u32[]{:S(2)}) copy-start(f32[1024]{0:T(1024)S(1)} %add_rsqrt_fusion) | copy-start | bytes 12292
  12.4 12.2 %copy-start.28 = (bf16[4096,1024]{1,0:T(8,128)(2,1)S(1)}, bf16[4096,1024]{1,0:T(8,128)(2,1)}, u32[]{:S(2)}) copy-start(bf16[4096,1024]{1,0:T(8,128)(2,1)} %param.33) | copy-start | bytes 25165828
  12.4 12.2 %copy-start.30 = (bf16[1024,3072]{1,0:T(8,128)(2,1)S(1)}, bf16[1024,3072]{1,0:T(8,128)(2,1)}, u32[]{:S(2)}) copy-start(bf16[1024,3072]{1,0:T(8,128)(2,1)} %param.27) | copy-start | bytes 18874372
  13.3 11.2 copy-start.10
  18.2 6.3 copy-start.13
  99.1 49.1 %copy-start.2 = (bf16[1024,1024]{1,0:T(8,128)(2,1)S(1)}, bf16[1024,1024]{1,0:T(8,128)(2,1)}, u32[]{:S(2)}) copy-start(bf16[1024,1024]{1,0:T(8,128)(2,1)} %get-tuple-element.217) | copy-start | bytes 6291460 | tf_op jit(solution)/shard_map/cond
  167.4 634.3 %reduce-scatter.5.cloned.1.call-start = ((), (), s32[]{:S(2)}) async-start(), calls=%async_computation.4 | async-start | bytes 12976128 | tf_op jit(solution)/shard_map/reduce_scatter | solution.py:337
  176.6 43.1 %copy-start.29 = (bf16[1024,4096]{1,0:T(8,128)(2,1)S(1)}, bf16[1024,4096]{1,0:T(8,128)(2,1)}, u32[]{:S(2)}) copy-start(bf16[1024,4096]{1,0:T(8,128)(2,1)} %get-tuple-element.226) | copy-start | bytes 25165828 | tf_op jit(solution)/shard_map/cond
  255.7 731.6 %reduce-scatter.9.cloned.1.call-start = ((), (), s32[]{:S(2)}) async-start(), calls=%async_computation.6 | async-start | bytes 17301504 | tf_op jit(solution)/shard_map/reduce_scatter | solution.py:341
  273.3 901.4 %reduce-scatter.11.cloned.1.call-start = ((), (), s32[]{:S(2)}) async-start(), calls=%async_computation.7 | async-start | bytes 17301504 | tf_op jit(solution)/shard_map/reduce_scatter | solution.py:343
  273.4 395.4 %copy-start = (bf16[1024,1024]{1,0:T(8,128)(2,1)S(1)}, bf16[1024,1024]{1,0:T(8,128)(2,1)}, u32[]{:S(2)}) copy-start(bf16[1024,1024]{1,0:T(8,128)(2,1)} %param.23) | copy-start | bytes 6291460
  277.9 399.4 %collective-permute-start.1 = (bf16[1024,1024]{1,0:T(8,128)(2,1)}, bf16[1024,1024]{1,0:T(8,128)(2,1)}, u32[]{:S(2)}, u32[]{:S(2)}) collective-permute-start(bf16[1024,1024]{1,0:T(8,128)(2,1)} %convert_element_type.134), channel_id=1, source_target_pairs={{0,1},{1,0},{2,3},{3,2},{4,5},{5,4},{6,7},{7,6},{8,9},{9,8},{10,11... | collective-permute-start | bytes 6291464 | tf_op jit(solution)/shard_map/ppermute | solution.py:19
  668.7 4.6 collective-permute-start
  671.3 11.8 %copy-start.25 = (f32[1024]{0:T(1024)S(1)}, f32[1024]{0:T(1024)}, u32[]{:S(2)}) copy-start(f32[1024]{0:T(1024)} %copy-done.24) | copy-start | bytes 12292
  671.3 11.8 %copy-start.27 = (f32[1024]{0:T(1024)S(1)}, f32[1024]{0:T(1024)}, u32[]{:S(2)}) copy-start(f32[1024]{0:T(1024)} %copy-done.26) | copy-start | bytes 12292
  671.3 57.6 %copy-start.20 = (f32[1024]{0:T(1024)S(1)}, f32[1024]{0:T(1024)}, u32[]{:S(2)}) copy-start(f32[1024]{0:T(1024)} %copy-done.19) | copy-start | bytes 12292
  671.3 57.6 %copy-start.22 = (f32[1024]{0:T(1024)S(1)}, f32[1024]{0:T(1024)}, u32[]{:S(2)}) copy-start(f32[1024]{0:T(1024)} %copy-done.21) | copy-start | bytes 12292
  671.3 57.6 %copy-start.23 = (f32[1024]{0:T(1024)S(1)}, f32[1024]{0:T(1024)}, u32[]{:S(2)}) copy-start(f32[1024]{0:T(1024)} %param.25) | copy-start | bytes 12292
  671.3 11.4 copy-start.1
  (3 other events, 7.7 us)
Sparse Core Ops, SparseCore 0:
  167.5 202.4 reduce-scatter.6
  376.6 425.0 reduce-scatter.4
  804.7 182.5 reduce-scatter.8
  990.2 184.4 reduce-scatter.10
where the time goes:
time: 1190 us; the launch traced here: 1180 us
  waiting for transfers between devices  441 us (37%)
  starting transfers between devices  390 us (33%)
  matrix products  147 us (12%)
  other arithmetic  85.8 us (7%)
  blocking collectives  42.2 us (4%)
  local copies, waits for them, and re-layouts  40.1 us (3%)
  loops' own time  21.4 us (2%)
  between operations  14.3 us (1%)
    ppermute x2, starting transfers between devices, partner_2(): lax.ppermute(array, axis, [(i, i ^ 1 << apart) for i in range(lax.axis_si...  390 us
    reduce_scatter x1, waiting for transfers between devices, body(): lax.psum_scatter(top_grads[2], ('dp', 'pair'), scatter_dimension=0, tiled...  187 us
    reduce_scatter x1, waiting for transfers between devices, body(): lax.psum_scatter(rest_grads[2], ('dp', 'pair'), scatter_dimension=0, tile...  186 us
    reduce_scatter x1, waiting for transfers between devices, body(): lax.psum_scatter(rest_grads[0], ('dp', 'pair'), scatter_dimension=0, tile...  65.5 us
    dot_general x1, matrix products, feed_top(): jnp.einsum('tf,te->fe', act_b, cotangent, preferred_element_type=jnp.floa...  46.6 us
    dot_general x1, matrix products, feed_forward(): jnp.dot(act_b, fc_out_weight, preferred_element_type=jnp.float32)  45.6 us
    reduce_sum x1, other arithmetic, feed_rest(): in_b_grad = jnp.sum(d_pre, axis=0, dtype=jnp.float32)  43.1 us
    unnamed x1, blocking collectives  42.2 us
  transfers between devices with their start and end apart: 6, of which 4 were waited for; matrix products, arithmetic and copies ran while one was open for 10% of the time, Pallas kernels for 0%

commit v1 on v0

v1 whole, which is shorter than its diff:
```python
from functools import partial

import jax
import jax.numpy as jnp
import numpy as np
from jax import lax
from jax.experimental import pallas as pl
from jax.experimental.pallas import tpu as pltpu
from jax.sharding import PartitionSpec as P

F32, BF = jnp.float32, jnp.bfloat16
MESH = pl.DeviceIdType.MESH
EPS = 1e-05
SEQ, D, FF, HEAD, ROT, DOCS = 1024, 1024, 4096, 64, 16, 8
INNER = 16
ORDER_A, ORDER_B = (0, 2, 1, 3), (1, 2, 0, 3)
LAGS = (1, 2, 3, 4)


def dot(a, b):
    return lax.dot_general(a, b, (((1,), (0,)), ((), ())), preferred_element_type=F32)


def dot_t(a, b):
    return lax.dot_general(a, b, (((1,), (1,)), ((), ())), preferred_element_type=F32)


def t_dot(a, b):
    return lax.dot_general(a, b, (((0,), (0,)), ((), ())), preferred_element_type=F32)


def loop(n, body, first=0):
    def step(i, c):
        body(i)
        return c

    lax.fori_loop(first, n, step, 0)


def at_multiple(start, size, of=None):
    return pl.ds(pl.multiple_of(start, of or size), size)


class Scope:
    pass


SCRATCH = (
    ("A", (3, SEQ, D), BF),
    ("ACC", (2, SEQ, D), F32),
    ("WA", (2, D, 768), BF),
    ("WB", (D, D), BF),
    ("PD", (SEQ, 512), F32),
    ("QKV", (SEQ, 768), BF),
    ("DR", (SEQ, 768), BF),
    ("GW", (16, 2, 2, 2, 2, 64, 256), BF),
    ("RW1", (16, 2, 2, 2, 64, 256), BF),
    ("RW2", (16, 2, 2, 64, 256), BF),
    ("RW3", (16, 2, 64, 256), BF),
    ("RW4", (16, 64, 256), BF),
    ("GO", (16, 256, D), BF),
    ("RO1A", (8, 256, 512), BF),
    ("RO2A", (4, 256, 512), BF),
    ("RO3A", (2, 256, 512), BF),
    ("RO4A", (256, 512), BF),
    ("RO1B", (4, 2, 256, 512), BF),
    ("RO2B", (2, 2, 256, 512), BF),
    ("RO3B", (2, 256, 512), BF),
    ("RO4B", (256, 512), BF),
    ("bcol", (8, 4096), F32),
    ("bsum", (8, D), F32),
    ("lnsum", (2, 8, D), F32),
    ("VEC", (8, D), F32),
    ("VRECV", (4, 8, D), F32),
    ("VPART", (8, D), F32),
)
SEMS = (
    ("lsem", (2, 2)),
    ("hsem", (6,)),
    ("qsem", (2, 3)),
    ("ws", (16, 4)),
    ("wr", (16, 4)),
    ("os", (8, 2, 4)),
    ("orr", (8, 2, 4)),
    ("vs", (5,)),
    ("vr", (5,)),
    ("xs", (4,)),
    ("xr", (4,)),
    ("fs", (5,)),
    ("fr", (5,)),
    ("fl", (7,)),
)
INPUTS = ("hidden", "lens", "gain", "shift", "w_qkv", "b_qkv", "w_dense", "b_dense", "w_in", "b_in", "w_out", "b_out", "cot")
OUTPUTS = ("o_out", "o_ig", "o_qkv", "o_dense", "o_in", "o_outw", "o_vec")


class Reducer:
    def __init__(self, s, extra):
        self.s, self.extra = s, extra
        dp = lax.axis_index("dp")
        inner = dp // extra
        self.dp, self.pr = dp, lax.axis_index("pair")
        self.bits = [inner % 2, (inner // 2) % 2, (inner // 4) % 2, inner // 8]
        self.partner = [dp + (1 - 2 * self.bits[b]) * (extra << b) for b in range(4)]

    def to(self, src, dst, ss, rs, b):
        return pltpu.make_async_remote_copy(
            src_ref=src, dst_ref=dst, send_sem=ss, recv_sem=rs, device_id=(self.partner[b], self.pr), device_id_type=MESH
        )

    def w_half(self, order, st, u, bit):
        s = self.s
        if st == 0:
            return s.GW.at[u, :, :, :, bit] if order == ORDER_A else s.GW.at[u, :, :, bit]
        if st == 1:
            return s.RW1.at[u, :, bit]
        if st == 2:
            return s.RW2.at[u, :, bit]
        return s.RW3.at[u, bit]

    def w_copy(self, order, st, u):
        s, b = self.s, order[st]
        dst = (s.RW1, s.RW2, s.RW3, s.RW4)[st].at[u]
        return self.to(self.w_half(order, st, u, 1 - self.bits[b]), dst, s.ws.at[u, st], s.wr.at[u, st], b)

    def w_finish(self, order, st, u, col):
        s, b = self.s, order[st]
        self.w_copy(order, st, u).wait_recv()
        kept = self.w_half(order, st, u, self.bits[b])
        got = (s.RW1, s.RW2, s.RW3, s.RW4)[st].at[u]
        if st < 3:
            lead = got.shape[0]
            for i in range(lead):
                got[i] = (got[i].astype(F32) + kept[i].astype(F32)).astype(BF)
            self.w_copy(order, st + 1, u).start()
        else:
            rows, lanes = at_multiple(64 * (col // 1024), 64), at_multiple(lax.rem(col, 1024), 256)
            s.ACC[0, rows, lanes] = got[...].astype(F32) + kept[...].astype(F32)

    def o_bits(self, c):
        return {1: c % 2, 2: (c // 2) % 2, 3: c // 4}

    def o_plan(self, order, st, c):
        s, x = self.s, self.bits[0]
        own = self.o_bits(c)
        same = {b: self.bits[b] == own[b] for b in (1, 2, 3)}
        zc, yc, hc = (c // 2) % 2, c % 2, c // 4
        n = 0 if order == ORDER_A else 1
        sems = (s.os.at[c, n, st], s.orr.at[c, n, st])
        everyone = c >= 0
        if order == ORDER_A:
            lanes = pl.ds(0, 512)
            if st == 0:
                return everyone, everyone, self.to(s.GO.at[2 * c + 1 - x, :, lanes], s.RO1A.at[c], *sems, 0), s.RO1A.at[c]
            if st == 1:
                dst = s.RO2A.at[2 * hc + yc]
                return everyone, same[2], self.to(s.RO1A.at[c], dst, *sems, 2), dst
            if st == 2:
                dst = s.RO3A.at[hc]
                return same[2], same[2] & same[1], self.to(s.RO2A.at[2 * hc + yc], dst, *sems, 1), dst
            part = same[2] & same[1]
            return part, part & same[3], self.to(s.RO3A.at[hc], s.RO4A, *sems, 3), s.RO4A
        lanes = pl.ds(512, 512)
        if st == 0:
            dst = s.RO1B.at[c // 2]
            return everyone, same[1], self.to(s.GO.at[pl.ds(2 * c, 2), :, lanes], dst, *sems, 1), dst
        if st == 1:
            dst = s.RO2B.at[hc]
            return same[1], same[1] & same[2], self.to(s.RO1B.at[c // 2], dst, *sems, 2), dst
        part = same[1] & same[2]
        if st == 2:
            dst = s.RO3B.at[hc]
            return part, part, self.to(s.RO2B.at[hc, 1 - x], dst, *sems, 0), dst
        return part, part & same[3], self.to(s.RO3B.at[hc], s.RO4B, *sems, 3), s.RO4B

    def o_sends(self, order, st):
        return (order == ORDER_A and st == 0) or (order == ORDER_B and st == 2)

    def o_start(self, order, st, c):
        part, takes, copy, _ = self.o_plan(order, st, c)
        if self.o_sends(order, st):
            pl.when(part)(lambda: copy.start())
        else:
            pl.when(part & jnp.logical_not(takes))(lambda: copy.start())

    def o_wait_sent(self, order, st, c):
        part, takes, copy, _ = self.o_plan(order, st, c)
        if self.o_sends(order, st):
            pl.when(part)(lambda: copy.wait_send())
        else:
            pl.when(part & jnp.logical_not(takes))(lambda: copy.wait_send())

    def o_finish(self, order, st, c):
        s, x = self.s, self.bits[0]
        _, takes, copy, got = self.o_plan(order, st, c)
        zc, yc, hc = (c // 2) % 2, c % 2, c // 4
        lanes = pl.ds(0, 512) if order == ORDER_A else pl.ds(512, 512)
        if order == ORDER_A:
            kept = (s.GO.at[2 * c + x, :, lanes], s.RO1A.at[c], s.RO2A.at[2 * hc + yc], s.RO3A.at[hc])[st]
        else:
            kept = (s.GO.at[pl.ds(2 * c, 2), :, lanes], s.RO1B.at[c // 2], s.RO2B.at[hc, x], s.RO3B.at[hc])[st]

        @pl.when(takes)
        def _():
            copy.wait_recv()
            if st == 3:
                s.ACC[0, 256:512, lanes] = got[...].astype(F32) + kept[...].astype(F32)
            elif len(got.shape) == 3:
                for i in range(2):
                    got[i] = (got[i].astype(F32) + kept[i].astype(F32)).astype(BF)
            else:
                got[...] = (got[...].astype(F32) + kept[...].astype(F32)).astype(BF)

        if st < 3:
            self.o_start(order, st + 1, c)


def layer_norm(load_rows, gain, shift, nb):
    def tile(i):
        x = load_rows(i).astype(F32)
        mean = jnp.mean(x, axis=1, keepdims=True)
        cen = x - mean
        inv = lax.rsqrt(jnp.mean(cen * cen, axis=1, keepdims=True) + EPS)
        nb[at_multiple(i * 128, 128), :] = (cen * inv * gain + shift).astype(BF)

    loop(8, tile)


A1, A2, A3, A4, A5 = 0.254829592, -0.284496736, 1.421413741, -1.453152027, 1.061405429


def gelu_both(x):
    e = jnp.exp(-0.5 * (x * x))
    t = 1.0 / (1.0 + (0.3275911 * 0.7071067811865476) * jnp.abs(x))
    poly = ((((0.5 * A5) * t + (0.5 * A4)) * t + (0.5 * A3)) * t + (0.5 * A2)) * t + (0.5 * A1)
    q = poly * t * e
    cdf = jnp.where(x >= 0, 1.0 - q, q)
    return cdf, x * (e * 0.3989422804014327)


def load_inputs(s):
    hc = [pltpu.make_async_copy(s.hidden.at[pl.ds(256 * j, 256)], s.GO.at[12 + j], s.hsem.at[j]) for j in range(4)]
    gc = pltpu.make_async_copy(s.cot, s.A.at[1], s.hsem.at[4])
    for cp in hc:
        cp.start()
    gc.start()
    return hc, gc


def staged_rows(s):
    return lambda i: s.GO[12 + i // 2, at_multiple(128 * lax.rem(i, 2), 128), :]


def feed_role(s, rs, enter):
    nb, g = s.A.at[0], s.A.at[1]
    dn, out = s.ACC.at[0], s.ACC.at[1]

    def weights(c, slot):
        cols = at_multiple(c * 512, 512)
        return (
            pltpu.make_async_copy(s.w_in.at[:, cols], s.WA.at[slot, :, pl.ds(0, 512)], s.lsem.at[0, slot]),
            pltpu.make_async_copy(s.w_out.at[cols, :], s.WB.at[at_multiple(512 * slot, 512)], s.lsem.at[1, slot]),
        )

    hc, gc = load_inputs(s)
    for cp in weights(0, 0):
        cp.start()
    for cp in hc:
        cp.wait()
    layer_norm(staged_rows(s), s.gain[...], s.shift[...], nb)
    gc.wait()
    s.bsum[...] = jnp.zeros((8, D), F32)

    def prepare(i):
        at = at_multiple(i * 128, 128)
        s.bsum[...] += jnp.sum(g[at, :].astype(F32).reshape(16, 8, D), axis=0)
        dn[at, :] = jnp.zeros((128, D), F32)
        out[at, :] = jnp.zeros((128, D), F32)

    loop(8, prepare)
    enter()

    def progress(t):
        @pl.when(t < 8)
        def _():
            rs.w_copy(ORDER_A, 0, 2 * t).start()
            rs.w_copy(ORDER_B, 0, 2 * t + 1).start()
            rs.o_start(ORDER_A, 0, t)
            rs.o_start(ORDER_B, 0, t)

        for st in range(3):
            c = t - LAGS[st]

            @pl.when((c >= 0) & (c < 8))
            def _(st=st, c=c):
                rs.w_finish(ORDER_A, st, 2 * c, 512 * c)
                rs.w_finish(ORDER_B, st, 2 * c + 1, 512 * c + 256)
                rs.o_finish(ORDER_A, st, c)
                rs.o_finish(ORDER_B, st, c)

    def chunk(c):
        slot = lax.rem(c, 2)

        @pl.when(c < 7)
        def _():
            for cp in weights(c + 1, 1 - slot):
                cp.start()

        for cp in weights(c, slot):
            cp.wait()
        win, wout = s.WA.at[slot, :, pl.ds(0, 512)], s.WB.at[at_multiple(512 * slot, 512)]
        cols = at_multiple(c * 512, 512)
        bias = s.b_in[:, cols]
        bacc = jnp.zeros((8, 512), F32)
        for rt in range(2):
            rows = pl.ds(512 * rt, 512)
            s.PD[0:512, :] = dot(nb[rows, :], win[...]) + bias
            s.PD[512:1024, :] = dot_t(g[rows, :], wout[...])
            for q in range(4):
                r, r2, ro = pl.ds(128 * q, 128), pl.ds(512 + 128 * q, 128), pl.ds(512 * rt + 128 * q, 128)
                pre = s.PD[r, :]
                cdf, xphi = gelu_both(pre)
                s.QKV[ro, 0:512] = (pre * cdf).astype(BF)
                dp = (s.PD[r2, :] * (cdf + xphi)).astype(BF)
                s.DR[ro, 0:512] = dp
                bacc = bacc + jnp.sum(dp.astype(F32).reshape(16, 8, 512), axis=0)
            for h in range(2):
                part = pl.ds(512 * rt + 256 * h, 256)
                out[part, :] += dot(s.QKV[part, 0:512], wout[...])
                dn[part, :] += dot_t(s.DR[part, 0:512], win[...])
        s.bcol[:, cols] = bacc
        for q in range(4):
            tile = t_dot(nb[:, pl.ds(256 * q, 256)], s.DR[:, 0:512]).astype(BF)
            for i in range(2):
                s.GW[2 * c + i, q // 2, q % 2] = tile[:, 256 * i : 256 * i + 256].reshape(2, 2, 64, 256)
        for i in range(2):
            s.GO[2 * c + i] = t_dot(s.QKV[:, 256 * i : 256 * i + 256], g[...]).astype(BF)
        progress(c)

    loop(8, chunk)
    for j in range(4):
        s.VEC[j : j + 1, :] = jnp.sum(s.bcol[:, 1024 * j : 1024 * j + 1024], axis=0, keepdims=True)
    s.VEC[4:5, :] = jnp.sum(s.bsum[...], axis=0, keepdims=True)
    s.VEC[5:8, :] = jnp.zeros((3, D), F32)

    def finish_all():
        def units(c):
            rs.w_finish(ORDER_A, 3, 2 * c, 512 * c)
            rs.w_finish(ORDER_B, 3, 2 * c + 1, 512 * c + 256)
            rs.o_finish(ORDER_A, 3, c)
            rs.o_finish(ORDER_B, 3, c)

        loop(8, units)

    def wait_sent():
        def units(c):
            for st in range(4):
                rs.w_copy(ORDER_A, st, 2 * c).wait_send()
                rs.w_copy(ORDER_B, st, 2 * c + 1).wait_send()
                rs.o_wait_sent(ORDER_A, st, c)
                rs.o_wait_sent(ORDER_B, st, c)

        loop(8, units)

    return progress, finish_all, wait_sent


def attention_role(s, rs, enter):
    nb, g, dcT = s.A.at[0], s.A.at[1], s.A.at[2]
    dn, S1 = s.ACC.at[0], s.ACC.at[1]

    def weights(gr, slot):
        return [
            pltpu.make_async_copy(
                s.w_qkv.at[:, at_multiple(j * 1024 + gr * 256, 256)], s.WA.at[slot, :, pl.ds(256 * j, 256)], s.qsem.at[slot, j]
            )
            for j in range(3)
        ]

    hc, gc = load_inputs(s)
    for cp in weights(0, 0):
        cp.start()
    dc = pltpu.make_async_copy(s.w_dense, s.WB, s.lsem.at[1, 0])
    dc.start()
    place = lax.broadcasted_iota(jnp.int32, (8, SEQ), 1)
    start = jnp.zeros((8, SEQ), jnp.int32)
    end = jnp.int32(0)
    for d in range(DOCS - 1):
        end = end + s.lens[0, d]
        start = jnp.where(place >= end, end, start)
    inv = np.float32(10000.0) ** (-(np.arange(0, ROT, 2, dtype=np.float32) / np.float32(ROT)))
    row = lax.broadcasted_iota(jnp.int32, (8, SEQ), 0)
    freq = jnp.zeros((8, SEQ), F32)
    for j in range(8):
        freq = jnp.where(row == j, float(inv[j]), freq)
    ang = (place - start).astype(F32) * freq
    co, si = jnp.cos(ang), jnp.sin(ang)
    one, zero = jnp.ones((48, SEQ), F32), jnp.zeros((48, SEQ), F32)
    for j, parts in enumerate(([co, co, one, co, co, one], [-si, si, zero, -si, si, zero])):
        table = jnp.concatenate(parts, axis=0).T
        for i in range(4):
            S1[768:1024, 256 * i + 128 * j : 256 * i + 128 * j + 128] = table[256 * i : 256 * i + 256]
    blocks = [(qb, kb) for qb in range(4) for kb in range(max(0, qb - 2), qb + 1)]

    def mask_at(qb, kb):
        n = blocks.index((qb, kb))
        return s.GO.at[8 + n // 4, :, pl.ds(256 * (n % 4), 256)]

    for qb, kb in blocks:
        kidx = lax.broadcasted_iota(jnp.int32, (256, 256), 0) + 256 * kb
        qidx = lax.broadcasted_iota(jnp.int32, (256, 256), 1) + 256 * qb
        st = start[0:1, 256 * qb : 256 * qb + 256]
        mask_at(qb, kb)[...] = jnp.where((kidx >= st) & (kidx <= qidx), 0.0, -1e9).astype(BF)
    for cp in hc:
        cp.wait()
    layer_norm(staged_rows(s), s.gain[...], s.shift[...], nb)
    gc.wait()
    dc.wait()
    s.bsum[...] = jnp.zeros((8, D), F32)

    def d_context(i):
        at = at_multiple(i * 512, 512)
        for q in range(4):
            dcT[pl.ds(256 * q, 256), at] = dot_t(s.WB[pl.ds(256 * q, 256), :], g[at, :]).astype(BF)
        s.bsum[...] += jnp.sum(g[at, :].astype(F32).reshape(64, 8, D), axis=0)
        dn[at, :] = jnp.zeros((512, D), F32)

    loop(2, d_context)
    enter()
    E = lambda n: s.GO.at[n]
    DS = lambda n: s.GO.at[3 + n]
    kT, vT = s.GO.at[6], s.GO.at[7]
    ones = jnp.ones((16, SEQ), BF)
    lane = lax.broadcasted_iota(jnp.int32, (256, 256), 1)

    def turn(x, i, sign):
        cosines, sines = (S1[768:1024, at_multiple(256 * i + 128 * j, 128)] for j in range(2))
        low = lax.broadcasted_iota(jnp.int32, (256, 128), 1) % 64 < 8
        parts = []
        for j in range(x.shape[1] // 128):
            u = x[:, 128 * j : 128 * j + 128]
            a = jnp.where(low, pltpu.roll(u, 120, 1), pltpu.roll(u, 8, 1)) * sines
            parts.append(u * cosines + a if sign > 0 else u * cosines - a)
        return jnp.concatenate(parts, axis=1)

    def stack(x):
        zb = jnp.zeros_like(x)
        return jnp.concatenate([jnp.where((lane >= 64 * h) & (lane < 64 * h + 64), x, zb) for h in range(4)], axis=0)

    def diag(x):
        return jnp.concatenate([x[64 * h : 64 * h + 64, 256 * h : 256 * h + 256] for h in range(4)], axis=0)

    def rows4(x):
        return jnp.concatenate([jnp.broadcast_to(x[:, 256 * h : 256 * h + 256], (64, 256)) for h in range(4)], axis=0)

    def sum4(x):
        return jnp.concatenate([jnp.sum(x[64 * h : 64 * h + 64], axis=0, keepdims=True) for h in range(4)], axis=1)

    def finish(gr, st):
        @pl.when(gr >= 0)
        def _():
            rs.w_finish(ORDER_A, st, 3 * gr, 256 * gr)
            rs.w_finish(ORDER_B, st, 3 * gr + 1, 1024 + 256 * gr)
            rs.w_finish(ORDER_A, st, 3 * gr + 2, 2048 + 256 * gr)

    def group(gr):
        slot = lax.rem(gr, 2)

        @pl.when(gr < 3)
        def _():
            for cp in weights(gr + 1, 1 - slot):
                cp.start()

        for cp in weights(gr, slot):
            cp.wait()
        w = s.WA.at[slot]
        bq = jnp.concatenate([s.b_qkv[:, at_multiple(1024 * j + gr * 256, 256)] for j in range(3)], axis=1)

        def project(i):
            for h in range(2):
                at = at_multiple(i * 512 + 256 * h, 256)
                part = dot(nb[at, :], w[...]) + bq
                s.QKV[at, 0:256] = turn(part[:, 0:256], 2 * i + h, 1).astype(BF) * BF(0.125)
                s.QKV[at, 256:512] = turn(part[:, 256:512], 2 * i + h, 1).astype(BF)
                s.QKV[at, 512:768] = part[:, 512:768].astype(BF)

        loop(2, project)
        crow = at_multiple(gr * 256, 256)
        for i in range(4):
            at = pl.ds(256 * i, 256)
            kT[:, at] = s.QKV[at, 256:512].astype(F32).T.astype(BF)
            vT[:, at] = s.QKV[at, 512:768].astype(F32).T.astype(BF)
        s.PD[...] = jnp.zeros((SEQ, 512), F32)
        for qb in range(4):
            if qb < 3:
                finish(gr - 1, qb)
            qs = pl.ds(256 * qb, 256)
            kbs = list(range(max(0, qb - 2), qb + 1))
            nk = len(kbs)
            win = pl.ds(256 * kbs[0], 256 * nk)
            qst = stack(s.QKV[qs, 0:256])
            m = None
            for n, kb in enumerate(kbs):
                b = mask_at(qb, kb)[...].astype(F32)
                sc = dot_t(s.QKV[pl.ds(256 * kb, 256), 256:512], qst) + jnp.concatenate([b] * 4, axis=1)
                S1[pl.ds(256 * n, 256), :] = sc
                top = jnp.max(sc, axis=0, keepdims=True)
                m = top if m is None else jnp.maximum(m, top)
            for n in range(nk):
                E(n)[...] = jnp.exp(S1[pl.ds(256 * n, 256), :] - m).astype(BF)
            ev = s.GO[0:nk].reshape(256 * nk, D)
            cx = dot(jnp.concatenate([vT[:, win], ones[:, 0 : 256 * nk]], axis=0), ev)
            li = 1.0 / cx[256:257, :]
            lsel = rows4(li)
            cT = diag(cx) * lsel
            dcs = (dcT[crow, qs].astype(F32) * lsel).astype(BF).astype(F32)
            dcT[crow, qs] = cT.astype(BF)
            inner = sum4(cT * dcs)
            dst = stack(dcs.T.astype(BF))
            for n, kb in enumerate(kbs):
                ks = pl.ds(256 * kb, 256)
                dP = dot_t(s.QKV[ks, 512:768], dst)
                DS(n)[...] = (E(n)[...].astype(F32) * (dP - inner)).astype(BF)
                s.PD[ks, 0:256] += dot(DS(n)[...], qst)
                s.PD[ks, 256:512] += dot(E(n)[...], dst)
            dq = diag(dot(kT[:, win], s.GO[3 : 3 + nk].reshape(256 * nk, D)))
            s.DR[qs, 0:256] = turn(dq.T * 0.125, qb, -1).astype(BF)
        for i in range(4):
            at = pl.ds(256 * i, 256)
            s.DR[at, 256:512] = turn(s.PD[at, 0:256], i, -1).astype(BF)
        s.DR[:, 512:768] = s.PD[:, 256:512].astype(BF)
        for q in range(4):
            tile = t_dot(nb[:, pl.ds(256 * q, 256)], s.DR[...]).astype(BF)
            for j in range(3):
                s.GW[3 * gr + j, q // 2, q % 2] = tile[:, 256 * j : 256 * j + 256].reshape(2, 2, 64, 256)
        rs.w_copy(ORDER_A, 0, 3 * gr).start()
        rs.w_copy(ORDER_B, 0, 3 * gr + 1).start()
        rs.w_copy(ORDER_A, 0, 3 * gr + 2).start()
        for j in range(3):
            s.bcol[:, at_multiple(1024 * j + gr * 256, 256)] = jnp.sum(
                s.DR[:, 256 * j : 256 * j + 256].astype(F32).reshape(128, 8, 256), axis=0
            )

        def d_normed(i):
            for h in range(2):
                at = at_multiple(i * 512 + 256 * h, 256)
                dn[at, :] += dot_t(s.DR[at, :], w[...])

        loop(2, d_normed)

    loop(4, group)

    for q in range(4):
        tile = dot(dcT[pl.ds(256 * q, 256), :], g[...]).astype(BF)
        for j in range(4):
            s.GW[12 + j, q // 2, q % 2] = tile[:, 256 * j : 256 * j + 256].reshape(2, 2, 64, 256)
    for j in range(4):
        rs.w_copy(ORDER_B, 0, 12 + j).start()

    def context_rows(i):
        at = at_multiple(i * 128, 128)
        nb[:, at] = dcT[at, :].astype(F32).T.astype(BF)

    loop(8, context_rows)
    for i in range(4):
        at = pl.ds(256 * i, 256)
        S1[at, :] = dot(nb[at, :], s.WB[...])
    for j in range(3):
        s.VEC[j : j + 1, :] = jnp.sum(s.bcol[:, 1024 * j : 1024 * j + 1024], axis=0, keepdims=True)
    s.VEC[3:4, :] = jnp.sum(s.bsum[...], axis=0, keepdims=True)
    s.VEC[6:8, :] = jnp.zeros((2, D), F32)

    def progress(t):
        if t < 11:
            finish(3, t - 8)
            for j in range(4):
                rs.w_finish(ORDER_B, t - 8, 12 + j, 3072 + 256 * j)

    def finish_all():
        def units(gr):
            finish(gr, 3)
            rs.w_finish(ORDER_B, 3, 12 + gr, 3072 + 256 * gr)

        loop(4, units)

    def wait_sent():
        def units(gr):
            for st in range(4):
                rs.w_copy(ORDER_A, st, 3 * gr).wait_send()
                rs.w_copy(ORDER_B, st, 3 * gr + 1).wait_send()
                rs.w_copy(ORDER_A, st, 3 * gr + 2).wait_send()
                rs.w_copy(ORDER_B, st, 12 + gr).wait_send()

        loop(4, units)

    return progress, finish_all, wait_sent


def kernel(extra, *refs):
    s = Scope()
    names = INPUTS + OUTPUTS + tuple(n for n, *_ in SCRATCH) + tuple(n for n, *_ in SEMS) + ("ready",)
    for n, r in zip(names, refs, strict=True):
        setattr(s, n, r)
    rs = Reducer(s, extra)
    pr, dp = rs.pr, rs.dp
    other = (dp, 1 - pr)
    barrier = pltpu.get_barrier_semaphore()
    for b in range(4):
        pl.semaphore_signal(barrier, inc=1, device_id=(rs.partner[b], pr), device_id_type=MESH)
    pl.semaphore_signal(barrier, inc=1, device_id=other, device_id_type=MESH)
    enter = lambda: pl.semaphore_wait(barrier, 5)

    def to_other(src, dst, ss, sr):
        return pltpu.make_async_remote_copy(src_ref=src, dst_ref=dst, send_sem=ss, recv_sem=sr, device_id=other, device_id_type=MESH)

    def role(is_attention, run, bias):
        progress, finish_all, wait_sent = run(s, rs, enter)
        own_half = 0 if is_attention else 1
        mine, theirs = pl.ds(512 * own_half, 512), pl.ds(512 * (1 - own_half), 512)
        pl.semaphore_signal(s.ready, inc=1, device_id=other, device_id_type=MESH)
        hc = pltpu.make_async_copy(s.hidden, s.A.at[2], s.hsem.at[5])
        hc.start()
        branch = s.A.at[0]

        def pack(i):
            at = at_multiple(i * 128, 128)
            branch[at, :] = (s.ACC[1, at, :] + bias[...]).astype(BF)

        loop(8, pack)

        def pack_dn(i):
            at = at_multiple(i * 128, 128)
            s.WB[at, :] = s.ACC[0, at, :].astype(BF)

        loop(8, pack_dn)
        progress(8)
        pl.semaphore_wait(s.ready, 1)
        moves = [
            to_other(branch.at[theirs, pl.ds(0, 512)], s.WA.at[1, pl.ds(0, 512), pl.ds(256, 512)], s.xs.at[0], s.xr.at[0]),
            to_other(branch.at[theirs, pl.ds(512, 512)], s.WA.at[1, pl.ds(512, 512), pl.ds(256, 512)], s.xs.at[1], s.xr.at[1]),
            to_other(s.WB.at[:, pl.ds(0, 768)], s.WA.at[0], s.xs.at[2], s.xr.at[2]),
            to_other(s.WB.at[:, pl.ds(768, 256)], s.WA.at[1, :, pl.ds(0, 256)], s.xs.at[3], s.xr.at[3]),
        ]
        for cp in moves:
            cp.start()
        progress(9)
        hc.wait()
        for cp in moves:
            cp.wait_recv()
        s.lnsum[...] = jnp.zeros((2, 8, D), F32)

        def last(i):
            at = at_multiple(i * 64, 64)
            x = s.A[2, at, :].astype(F32)
            mean = jnp.mean(x, axis=1, keepdims=True)
            cen = x - mean
            inv = lax.rsqrt(jnp.mean(cen * cen, axis=1, keepdims=True) + EPS)
            x_hat = cen * inv
            a = s.WB[at, :].astype(F32)
            b = jnp.concatenate([s.WA[0, at, :], s.WA[1, at, 0:256]], axis=1).astype(F32)
            dnv = (a + b).astype(BF).astype(F32)
            e = dnv * s.gain[...]
            grad = s.A[1, at, :].astype(F32) + inv * (
                e - jnp.mean(e, axis=1, keepdims=True) - x_hat * jnp.mean(e * x_hat, axis=1, keepdims=True)
            )
            if is_attention:
                s.lnsum[0] += jnp.sum((dnv * x_hat).reshape(8, 8, D), axis=0)
                s.lnsum[1] += jnp.sum(dnv.reshape(8, 8, D), axis=0)

            @pl.when(i // 8 == own_half)
            def _():
                here = 64 * lax.rem(i, 8)
                got = jnp.concatenate([s.WA[1, at_multiple(here, 64), 256:768], s.WA[1, at_multiple(512 + here, 64), 256:768]], axis=1)
                attn, mlp = (branch[at, :], got) if is_attention else (got, branch[at, :])
                branch[at, :] = (x + attn.astype(F32) + mlp.astype(F32)).astype(BF)

            s.A[2, at, :] = grad.astype(BF)

        loop(16, last)
        outs = [
            pltpu.make_async_copy(branch.at[mine], s.o_out, s.fl.at[0]),
            pltpu.make_async_copy(s.A.at[2], s.o_ig, s.fl.at[1]),
        ]
        for cp in outs:
            cp.start()
        if is_attention:
            for j in range(2):
                s.VEC[4 + j : 5 + j, :] = jnp.sum(s.lnsum[j], axis=0, keepdims=True)
        vecs = []
        for b in range(4):
            cp = rs.to(s.VEC, s.VRECV.at[b], s.vs.at[b], s.vr.at[b], b)
            cp.start()
            progress(10 + b)
            cp.wait()
            s.VEC[...] += s.VRECV[b]
        vx = to_other(s.VEC, s.VPART, s.vs.at[4], s.vr.at[4])
        vx.start()
        finish_all()

        def split(first, size, half):
            return pl.ds(first, size) if extra > 1 else pl.ds(first + half * (size // 2), size // 2)

        def pieces(attention, half):
            wide = [s.o_qkv.at[:, pl.ds(1024 * k, 1024)] for k in range(3)] + [s.o_dense]
            if not attention:
                wide = [s.o_in.at[:, pl.ds(1024 * k, 1024)] for k in range(4)]
            parts = [(s.ACC.at[0, split(64 * k, 64, half)], to) for k, to in enumerate(wide)]
            return parts if attention else parts + [(s.ACC.at[0, split(256, 256, half)], s.o_outw)]

        sent, local = [], []
        for n, (src, dst) in enumerate(pieces(is_attention, 1 - own_half)):
            cp = to_other(src, dst, s.fs.at[n], s.fr.at[n])
            cp.start()
            sent.append(cp)
        for n, (src, dst) in enumerate(pieces(is_attention, own_half)):
            cp = pltpu.make_async_copy(src, dst, s.fl.at[2 + n])
            cp.start()
            local.append(cp)
        vx.wait()
        s.o_vec[0 if is_attention else 1] = s.VEC[...]
        s.o_vec[1 if is_attention else 0] = s.VPART[...]
        wait_sent()
        for cp in moves:
            cp.wait_send()
        for cp in outs + local:
            cp.wait()
        for cp in sent:
            cp.wait_send()
        for n, (src, dst) in enumerate(pieces(not is_attention, own_half)):
            to_other(src, dst, s.fs.at[n], s.fr.at[n]).wait_recv()

    pl.when(pr == 0)(lambda: role(True, attention_role, s.b_dense))
    pl.when(pr == 1)(lambda: role(False, feed_role, s.b_out))


def call(extra, *args):
    rows = 32 if extra == 1 else 64
    outw = 128 if extra == 1 else 256
    anywhere, vmem, smem = (pl.BlockSpec(memory_space=m) for m in (pl.ANY, pltpu.VMEM, pltpu.SMEM))
    shapes = [
        ((512, D), BF), ((SEQ, D), BF), ((rows, 3072), F32), ((rows, D), F32), ((rows, FF), F32), ((outw, D), F32), ((2, 8, D), F32),
    ]
    return pl.pallas_call(
        partial(kernel, extra),
        out_shape=[jax.ShapeDtypeStruct(*x) for x in shapes],
        in_specs=[anywhere, smem, vmem, vmem, anywhere, vmem, anywhere, vmem, anywhere, vmem, anywhere, vmem, anywhere],
        out_specs=[anywhere] * 6 + [vmem],
        scratch_shapes=[pltpu.VMEM(shape, kind) for _, shape, kind in SCRATCH]
        + [pltpu.SemaphoreType.DMA(shape) for _, shape in SEMS]
        + [pltpu.SemaphoreType.REGULAR],
        compiler_params=pltpu.CompilerParams(collective_id=0, has_side_effects=True, vmem_limit_bytes=VMEM_LIMIT),
        cost_estimate=pl.CostEstimate(flops=50 * 10**9, bytes_accessed=40 * 10**6, transcendentals=10**7),
    )(*args)


VMEM_LIMIT = 62 * 2**20


def swap(x, bit):
    return lax.ppermute(x, "dp", [(i, i ^ bit) for i in range(lax.axis_size("dp"))])


def halve(x, bit):
    half = x.shape[0] // 2
    up = (lax.axis_index("dp") // bit) % 2
    keep = lax.dynamic_slice_in_dim(x, up * half, half, 0)
    give = lax.dynamic_slice_in_dim(x, (1 - up) * half, half, 0)
    return keep + swap(give, bit)


def body(hidden, doc_lengths, ln_gain, ln_bias, qkv_weight, qkv_bias, dense_weight, dense_bias, fc_in_weight, fc_in_bias, fc_out_weight, fc_out_bias, cotangent):
    extra = lax.axis_size("dp") // INNER
    output, input_grad, qkv, dense, w_in, w_out, vec = call(
        extra, hidden, doc_lengths, ln_gain[None], ln_bias[None], qkv_weight, qkv_bias[None], dense_weight, dense_bias[None],
        fc_in_weight, fc_in_bias[None], fc_out_weight, fc_out_bias[None], cotangent,
    )
    dp, pair = lax.axis_index("dp"), lax.axis_index("pair")
    if extra > 1:
        bit = extra // 2
        while bit:
            qkv, dense, w_in, w_out = (halve(x, bit) for x in (qkv, dense, w_in, w_out))
            vec = vec + swap(vec, bit)
            bit //= 2
        qkv, dense, w_in, w_out = (
            lax.dynamic_slice_in_dim(x, pair * (x.shape[0] // 2), x.shape[0] // 2, 0) for x in (qkv, dense, w_in, w_out)
        )
    place = dp * 2 + pair
    count = lax.axis_size("dp") * 2

    def own(x):
        x = x.reshape(-1)
        size = x.shape[0] // count
        return lax.dynamic_slice_in_dim(x, place * size, size, 0)

    return (
        output, input_grad, qkv, own(vec[0, 0:3]), dense, own(vec[0, 3]), w_in, own(vec[1, 0:4]), w_out, own(vec[1, 4]),
        own(vec[0, 4]), own(vec[0, 5]),
    )


def solution(mesh):
    rows = P("dp", None)
    shard, shard1 = P(("dp", "pair"), None), P(("dp", "pair"))
    return jax.shard_map(
        body,
        mesh=mesh,
        in_specs=(rows, rows) + (P(),) * 10 + (rows,),
        out_specs=(shard, rows, shard, shard1, shard, shard1, shard, shard1, shard, shard1, shard1, shard1),
        check_vma=False,
    )
```

time: 1190 us -> 185 us (0.16)
  waiting for transfers between devices: 441 us -> 0 us
  starting transfers between devices: 390 us -> 0 us
  Pallas kernels: 0 us -> 171 us
  matrix products: 147 us -> 0 us
  other arithmetic: 85.8 us -> 0 us
  blocking collectives: 42.2 us -> 0 us
  local copies, waits for them, and re-layouts: 40.1 us -> 11.5 us
  loops' own time: 21.4 us -> 0 us
  between operations: 14.3 us -> 0.69 us
    reduce_scatter x4 -> x0, waiting for transfers between devices: 438 us -> none  [the longest x1 187 us: body(): lax.psum_scatter(top_grads[2], ('dp', 'pair'), scatter_dimension=0, tiled...]
    ppermute x2 -> x0, starting transfers between devices: 390 us -> none  [partner_2(): lax.ppermute(array, axis, [(i, i ^ 1 << apart) for i in range(lax.axis_si...]
    pallas_call x0 -> x1, Pallas kernels: none -> 171 us  [call(): pl.pallas_call(partial(kernel, extra), out_shape=[jax.ShapeDtypeStruct(*x...]
    dot_general x6 -> x0, matrix products: 147 us -> none  [the longest x1 46.6 us: feed_top(): jnp.einsum('tf,te->fe', act_b, cotangent, preferred_element_type=jnp.floa...]
    reduce_sum x8 -> x0, other arithmetic: 53.3 us -> none  [the longest x1 43.1 us: feed_rest(): in_b_grad = jnp.sum(d_pre, axis=0, dtype=jnp.float32)]
    unnamed x1 -> x0, blocking collectives: 42.2 us -> none
    convert_element_type x7 -> x0, other arithmetic: 24.9 us -> none  [the longest x1 5.44 us: body(): (d_normed_own + d_normed_other).astype(jnp.bfloat16).astype(jnp.float32)]
    cond x5 -> x0, local copies, waits for them, and re-layouts: 17.6 us -> none  [the longest x1 17.5 us: body(): lax.cond(on_attention, attention_rest, feed_rest, d_context)]
  transfers between devices with their start and end apart: 6 -> 0, of which waited for: 4 -> 0; matrix products, arithmetic and copies ran while one was open for 10% -> 0% of each run, Pallas kernels for 0% -> 0%
where the time goes in v1:
time: 185 us; the launch traced here: 183 us
  Pallas kernels  171 us (92%)
  local copies, waits for them, and re-layouts  11.5 us (6%)
    pallas_call x1, Pallas kernels, call(): pl.pallas_call(partial(kernel, extra), out_shape=[jax.ShapeDtypeStruct(*x...  171 us
    unnamed x18, local copies, waits for them, and re-layouts  7.5 us

profile of v1, /device:TPU:3, one launch (start us, length us, event | category | flops | bytes accessed | tf_op | source)
XLA Modules:
  0.0 183.0 jit_solution(1845944830996793829)
XLA Ops:
  0.7 170.8 %shard_map.220 = (bf16[512,1024]{1,0:T(8,128)(2,1)}, bf16[1024,1024]{1,0:T(8,128)(2,1)}, f32[32,3072]{1,0:T(8,128)}, f32[32,1024]{1,0:T(8,128)}, f32[32,4096]{1,...) custom-call(bf16[1024,1024]{1,0:T(8,128)(2,1)} %refs_0_.1, s32[1,8]{1,0:T(1,128)} %refs_1_.1, f32[1,1024]{1,0:T(1,128)} %bitcast.22, ...), custom_call_target="tpu_custom_call" | custom-call | flops 49999998976 | bytes 40000000 | tf_op jit(solution)/shard_map/pallas_call | solution.py:743
  171.4 0.0 copy-start
  171.4 0.9 slice_bitcast_fusion
  172.4 0.6 dynamic_slice.29
  172.9 0.8 slice.18
  173.7 0.9 fusion.4
  174.6 0.6 dynamic_slice.26
  175.2 0.6 fusion.2
  175.8 0.6 fusion
  176.4 2.3 %copy.34 = bf16[512,1024]{1,0:T(8,128)(2,1)} copy(bf16[512,1024]{1,0:T(8,128)(2,1)} %get-tuple-element.46) | data formatting | bytes 2097152
  178.6 0.0 copy-done
  178.6 0.0 copy-start.3
  178.6 0.0 copy-start.4
  178.6 0.0 copy-start.2
  178.6 1.3 copy.35
  180.0 0.0 copy-done.3
  180.0 0.0 copy-start.1
  180.0 0.7 copy.36
  180.7 0.0 copy-done.4
  180.7 0.7 copy.37
  181.4 0.0 copy-done.2
  181.4 0.8 copy.38
  182.2 0.0 copy-done.1
  182.2 0.8 copy.39
  (2 shorter events, 0.0 us)
Async XLA Ops:
  171.4 7.2 %copy-start = (bf16[1024,1024]{1,0:T(8,128)(2,1)S(1)}, bf16[1024,1024]{1,0:T(8,128)(2,1)}, u32[]{:S(2)}) copy-start(bf16[1024,1024]{1,0:T(8,128)(2,1)} %get-tuple-element.47) | copy-start | bytes 6291460
  178.6 1.3 copy-start.3
  178.6 2.1 %copy-start.4 = (f32[32,1024]{1,0:T(8,128)S(1)}, f32[32,1024]{1,0:T(8,128)}, u32[]{:S(2)}) copy-start(f32[32,1024]{1,0:T(8,128)} %get-tuple-element.50) | copy-start | bytes 393220
  178.6 2.7 %copy-start.2 = (f32[32,4096]{1,0:T(8,128)S(1)}, f32[32,4096]{1,0:T(8,128)}, u32[]{:S(2)}) copy-start(f32[32,4096]{1,0:T(8,128)} %get-tuple-element.52) | copy-start | bytes 1572868
  180.0 2.2 %copy-start.1 = (f32[128,1024]{1,0:T(8,128)S(1)}, f32[128,1024]{1,0:T(8,128)}, u32[]{:S(2)}) copy-start(f32[128,1024]{1,0:T(8,128)} %get-tuple-element.54) | copy-start | bytes 1572868

commit v2 on v1

v2 whole, which is shorter than its diff:
```python
from functools import partial

import jax
import jax.numpy as jnp
import numpy as np
from jax import lax
from jax.experimental import pallas as pl
from jax.experimental.pallas import tpu as pltpu
from jax.sharding import PartitionSpec as P

F32, BF = jnp.float32, jnp.bfloat16
MESH = pl.DeviceIdType.MESH
EPS = 1e-05
SEQ, D, FF, HEAD, ROT, DOCS = 1024, 1024, 4096, 64, 16, 8
INNER = 16
X_FIRST, Y_FIRST, Z_FIRST, X_THEN_Z = (0, 1, 2, 3), (1, 0, 2, 3), (2, 1, 0, 3), (0, 2, 1, 3)
W_ORDERS = (X_FIRST, Y_FIRST)
O_ORDERS = (Z_FIRST, X_THEN_Z)
QKV_ORDERS = (X_FIRST, Y_FIRST, Z_FIRST)
DENSE_ORDERS = (Y_FIRST, Y_FIRST, Z_FIRST, X_FIRST)
LAGS = (1, 2, 3)


def dot(a, b):
    return lax.dot_general(a, b, (((1,), (0,)), ((), ())), preferred_element_type=F32)


def dot_t(a, b):
    return lax.dot_general(a, b, (((1,), (1,)), ((), ())), preferred_element_type=F32)


def t_dot(a, b):
    return lax.dot_general(a, b, (((0,), (0,)), ((), ())), preferred_element_type=F32)


def scoped(name, f):
    def g(*a, **k):
        with jax.named_scope(name):
            return f(*a, **k)
    return g


def loop(n, body, first=0):
    def step(i, c):
        body(i)
        return c

    lax.fori_loop(first, n, step, 0)


def at_multiple(start, size, of=None):
    return pl.ds(pl.multiple_of(start, of or size), size)


def xor(a, b):
    return a + b - 2 * a * b


class Scope:
    pass


SCRATCH = (
    ("A", (3, SEQ, D), BF),
    ("ACC", (2, SEQ, D), F32),
    ("WA", (2, D, 768), BF),
    ("WB", (D, D), BF),
    ("PD", (SEQ, 512), F32),
    ("GW", (16, 2, 2, 2, 2, 64, 256), BF),
    ("RW1", (16, 2, 2, 2, 64, 256), BF),
    ("RW2", (16, 2, 2, 64, 256), BF),
    ("RW3", (16, 2, 64, 256), BF),
    ("RW4", (16, 64, 256), BF),
    ("GO", (16, 256, D), BF),
    ("RO1", (2, 8, 2, 128, 512), BF),
    ("RO2", (2, SEQ, 512), BF),
    ("RO3", (SEQ, 512), BF),
    ("RO4", (2, 2, 128, 512), BF),
    ("bcol", (8, 4096), F32),
    ("bsum", (8, D), F32),
    ("lnsum", (2, 8, D), F32),
    ("VEC", (8, D), F32),
    ("VRECV", (6, 8, D), F32),
    ("VPART", (8, D), F32),
)
SEMS = (
    ("lsem", (2, 8)),
    ("hsem", (6,)),
    ("qsem", (2, 3)),
    ("ws", (16, 4)),
    ("wr", (16, 4)),
    ("os", (2, 8, 5)),
    ("orr", (2, 8, 5)),
    ("vs", (7,)),
    ("vr", (7,)),
    ("xs", (24,)),
    ("xr", (24,)),
    ("fs", (5,)),
    ("fr", (5,)),
    ("fl", (7,)),
)
INPUTS = ("hidden", "lens", "gain", "shift", "w_qkv", "b_qkv", "w_dense", "b_dense", "w_in", "b_in", "w_out", "b_out", "cot")
OUTPUTS = ("o_out", "o_ig", "o_qkv", "o_dense", "o_in", "o_outw", "o_vec")


class Reducer:
    def __init__(self, s, extra):
        self.s, self.extra = s, extra
        dp = lax.axis_index("dp")
        inner = dp // extra
        self.dp, self.pr = dp, lax.axis_index("pair")
        self.bits = [inner % 2, (inner // 2) % 2, (inner // 4) % 2, inner // 8]
        step = [(1 - 2 * self.bits[b]) * (extra << b) for b in range(4)]
        self.partner = [dp + step[b] for b in range(4)]
        self.lines = ((self.partner[2], self.partner[3], dp + step[2] + step[3]), (self.partner[0], self.partner[1], dp + step[0] + step[1]))

    def to(self, src, dst, ss, rs, b):
        return pltpu.make_async_remote_copy(
            src_ref=src, dst_ref=dst, send_sem=ss, recv_sem=rs, device_id=(self.partner[b], self.pr), device_id_type=MESH
        )

    def w_half(self, order, st, u, bit):
        s = self.s
        left = [b for b in (3, 2, 1, 0) if b not in order[:st]]
        ref = (s.GW, s.RW1, s.RW2, s.RW3)[st]
        return ref.at[(u,) + (slice(None),) * left.index(order[st]) + (bit,)]

    def w_copy(self, order, st, u):
        s, b = self.s, order[st]
        dst = (s.RW1, s.RW2, s.RW3, s.RW4)[st].at[u]
        return self.to(self.w_half(order, st, u, 1 - self.bits[b]), dst, s.ws.at[u, st], s.wr.at[u, st], b)

    def w_finish(self, order, st, u, cols):
        s, b = self.s, order[st]
        self.w_copy(order, st, u).wait_recv()
        kept = self.w_half(order, st, u, self.bits[b])
        got = (s.RW1, s.RW2, s.RW3, s.RW4)[st].at[u]
        if st < 3:
            lead = got.shape[0]
            for i in range(lead):
                got[i] = (got[i].astype(F32) + kept[i].astype(F32)).astype(BF)
            self.w_copy(order, st + 1, u).start()
        else:
            total = got[...].astype(F32) + kept[...].astype(F32)
            for i, at in enumerate(cols):
                s.ACC[0, at_multiple(64 * (at // 1024), 64), at_multiple(lax.rem(at, 1024), 128)] = total[:, 128 * i : 128 * i + 128]

    def chunk_of(self, c):
        return c % 2, (c // 2) % 2, c // 4

    def shard(self, c, x, y):
        a, b, _ = self.chunk_of(c)
        return x + 2 * y + 4 * xor(a, xor(x, y)) + 8 * xor(b, x)

    def ro2(self, n, c):
        return self.s.RO2.at[n, at_multiple(128 * c, 128)]

    def ro3(self, n, c):
        return self.s.RO3.at[at_multiple(512 * n + 128 * (c // 2), 128)]

    def o_shard(self, n, c, first, second):
        a, _, _ = self.chunk_of(c)
        p, q, r, _ = O_ORDERS[n]
        bit = {p: first, q: second, r: xor(a, xor(first, second))}
        return self.shard(c, bit[0], bit[1])

    def o_copies(self, n, st, c):
        s, own = self.s, self.bits
        a, b, h = self.chunk_of(c)
        p, q, r, _ = O_ORDERS[n]
        here = xor(a, xor(own[p], own[q])) == own[r]
        mine = here & (xor(b, own[0]) == own[3])

        def copy(src, dst, k, bit):
            return self.to(src, dst, s.os.at[n, c, k], s.orr.at[n, c, k], bit)

        if st == 0:
            copies = []
            for k in range(2):
                src = s.GO.at[self.o_shard(n, c, 1 - own[p], k), at_multiple(128 * h, 128), pl.ds(512 * n, 512)]
                copies.append(copy(src, s.RO1.at[n, c, k], k, p))
            return True, True, copies
        if st == 1:
            return True, True, [copy(s.RO1.at[n, c, 1 - own[q]], self.ro2(n, c), 2, q)]
        if st == 2:
            return jnp.logical_not(here), here, [copy(self.ro2(n, c), self.ro3(n, c), 3, r)]
        return here & jnp.logical_not(mine), mine, [copy(self.ro3(n, c), s.RO4.at[n, h], 4, 3)]

    def o_start(self, n, st, c):
        sends, _, copies = self.o_copies(n, st, c)

        @pl.when(sends)
        def _():
            for cp in copies:
                cp.start()

    def o_wait_sent(self, n, st, c):
        sends, _, copies = self.o_copies(n, st, c)

        @pl.when(sends)
        def _():
            for cp in copies:
                cp.wait_send()

    def o_finish(self, n, st, c):
        s, own = self.s, self.bits
        _, _, h = self.chunk_of(c)
        p, q, _, _ = O_ORDERS[n]
        lanes = pl.ds(512 * n, 512)
        _, takes, copies = self.o_copies(n, st, c)

        @pl.when(takes)
        def _():
            for cp in copies:
                cp.wait_recv()
            if st == 0:
                for k in range(2):
                    kept = s.GO[self.o_shard(n, c, own[p], k), at_multiple(128 * h, 128), lanes]
                    s.RO1[n, c, k] = (s.RO1[n, c, k].astype(F32) + kept.astype(F32)).astype(BF)
            elif st == 1:
                got = self.ro2(n, c)
                got[...] = (got[...].astype(F32) + s.RO1[n, c, own[q]].astype(F32)).astype(BF)
            elif st == 2:
                got = self.ro3(n, c)
                got[...] = (got[...].astype(F32) + self.ro2(n, c)[...].astype(F32)).astype(BF)
            else:
                s.ACC[0, at_multiple(256 + 128 * h, 128), lanes] = s.RO4[n, h].astype(F32) + self.ro3(n, c)[...].astype(F32)

        if st < 3:
            self.o_start(n, st + 1, c)


def layer_norm(load_rows, gain, shift, nb):
    def tile(i):
        x = load_rows(i).astype(F32)
        mean = jnp.mean(x, axis=1, keepdims=True)
        cen = x - mean
        inv = lax.rsqrt(jnp.mean(cen * cen, axis=1, keepdims=True) + EPS)
        nb[at_multiple(i * 128, 128), :] = (cen * inv * gain + shift).astype(BF)

    loop(8, tile)


A1, A2, A3, A4, A5 = 0.254829592, -0.284496736, 1.421413741, -1.453152027, 1.061405429


def gelu_both(x):
    e = jnp.exp(-0.5 * (x * x))
    t = 1.0 / (1.0 + (0.3275911 * 0.7071067811865476) * jnp.abs(x))
    poly = ((((0.5 * A5) * t + (0.5 * A4)) * t + (0.5 * A3)) * t + (0.5 * A2)) * t + (0.5 * A1)
    q = poly * t * e
    cdf = jnp.where(x >= 0, 1.0 - q, q)
    return cdf, x * (e * 0.3989422804014327)


def load_inputs(s):
    hc = [pltpu.make_async_copy(s.hidden.at[pl.ds(256 * j, 256)], s.GO.at[12 + j], s.hsem.at[j]) for j in range(4)]
    gc = pltpu.make_async_copy(s.cot, s.A.at[1], s.hsem.at[4])
    for cp in hc:
        cp.start()
    gc.start()
    return hc, gc


def staged_rows(s):
    return lambda i: s.GO[12 + i // 2, at_multiple(128 * lax.rem(i, 2), 128), :]


def feed_role(s, rs, enter):
    nb, g = s.A.at[0], s.A.at[1]
    dn, out = s.ACC.at[0], s.ACC.at[1]
    act, dpre = s.A.at[2, :, pl.ds(0, 512)], s.A.at[2, :, pl.ds(512, 512)]

    def units_at(c):
        return [256 * rs.shard(c, p % 2, p // 2) + 128 * (c // 4) for p in range(4)]

    def weights(c, slot):
        copies = []
        for p, at in enumerate(units_at(c)):
            cols, k = at_multiple(at, 128), 4 * slot + p
            copies.append(pltpu.make_async_copy(s.w_in.at[:, cols], s.WA.at[slot, :, pl.ds(128 * p, 128)], s.lsem.at[0, k]))
            copies.append(pltpu.make_async_copy(s.w_out.at[cols, :], s.WB.at[at_multiple(512 * slot + 128 * p, 128)], s.lsem.at[1, k]))
        return copies

    hc, gc = load_inputs(s)
    for cp in weights(0, 0):
        cp.start()
    for cp in hc:
        cp.wait()
    scoped('norm', layer_norm)(staged_rows(s), s.gain[...], s.shift[...], nb)
    gc.wait()
    s.bsum[...] = jnp.zeros((8, D), F32)

    def prepare(i):
        at = at_multiple(i * 128, 128)
        s.bsum[...] += jnp.sum(g[at, :].astype(F32).reshape(16, 8, D), axis=0)
        dn[at, :] = jnp.zeros((128, D), F32)
        out[at, :] = jnp.zeros((128, D), F32)

    scoped('prepare', loop)(8, prepare)
    enter()

    def progress(t):
        for st in (2, 1, 0):
            c = t - LAGS[st]

            @pl.when((c >= 0) & (c < 8))
            def _(st=st, c=c):
                rs.w_finish(W_ORDERS[0], st, 2 * c, None)
                rs.w_finish(W_ORDERS[1], st, 2 * c + 1, None)
                rs.o_finish(0, st, c)
                rs.o_finish(1, st, c)

    def chunk(c):
        slot = lax.rem(c, 2)

        @pl.when(c < 7)
        def _():
            for cp in weights(c + 1, 1 - slot):
                cp.start()

        for cp in weights(c, slot):
            cp.wait()
        win, wout = s.WA.at[slot, :, pl.ds(0, 512)], s.WB.at[at_multiple(512 * slot, 512)]
        places = units_at(c)
        bias = jnp.concatenate([s.b_in[:, at_multiple(at, 128)] for at in places], axis=1)
        bacc = jnp.zeros((8, 512), F32)
        for rt in range(2):
            rows = pl.ds(512 * rt, 512)
            s.PD[0:512, :] = dot(nb[rows, :], win[...]) + bias
            s.PD[512:1024, :] = dot_t(g[rows, :], wout[...])
            for q in range(4):
                r, r2, ro = pl.ds(128 * q, 128), pl.ds(512 + 128 * q, 128), pl.ds(512 * rt + 128 * q, 128)
                pre = s.PD[r, :]
                cdf, xphi = gelu_both(pre)
                act[ro, :] = (pre * cdf).astype(BF)
                dp = (s.PD[r2, :] * (cdf + xphi)).astype(BF)
                dpre[ro, :] = dp
                bacc = bacc + jnp.sum(dp.astype(F32).reshape(16, 8, 512), axis=0)
        for p, at in enumerate(places):
            s.bcol[:, at_multiple(at, 128)] = bacc[:, 128 * p : 128 * p + 128]
        for i in range(2):
            tile = t_dot(act[:, 256 * i : 256 * i + 256], g[...]).astype(BF)
            for p in range(2 * i, 2 * i + 2):
                s.GO[rs.shard(c, p % 2, p // 2), at_multiple(128 * (c // 4), 128), :] = tile[128 * (p % 2) : 128 * (p % 2) + 128]
        rs.o_start(0, 0, c)
        rs.o_start(1, 0, c)
        for q in range(4):
            tile = t_dot(nb[:, pl.ds(256 * q, 256)], dpre[...]).astype(BF)
            for i in range(2):
                s.GW[2 * c + i, q // 2, q % 2] = tile[:, 256 * i : 256 * i + 256].reshape(2, 2, 64, 256)
        rs.w_copy(W_ORDERS[0], 0, 2 * c).start()
        rs.w_copy(W_ORDERS[1], 0, 2 * c + 1).start()
        for h in range(4):
            part = pl.ds(256 * h, 256)
            out[part, :] += dot(act[part, :], wout[...])
            dn[part, :] += dot_t(dpre[part, :], win[...])
        scoped('reduce', progress)(c)

    loop(8, scoped('chunk', chunk))
    for j in range(4):
        s.VEC[j : j + 1, :] = jnp.sum(s.bcol[:, 1024 * j : 1024 * j + 1024], axis=0, keepdims=True)
    s.VEC[4:5, :] = jnp.sum(s.bsum[...], axis=0, keepdims=True)
    s.VEC[5:8, :] = jnp.zeros((3, D), F32)

    def finish_all():
        def units(c):
            places = units_at(c)
            rs.w_finish(W_ORDERS[0], 3, 2 * c, places[:2])
            rs.w_finish(W_ORDERS[1], 3, 2 * c + 1, places[2:])
            rs.o_finish(0, 3, c)
            rs.o_finish(1, 3, c)

        loop(8, units)

    def wait_sent():
        def units(c):
            for st in range(4):
                rs.w_copy(W_ORDERS[0], st, 2 * c).wait_send()
                rs.w_copy(W_ORDERS[1], st, 2 * c + 1).wait_send()
                rs.o_wait_sent(0, st, c)
                rs.o_wait_sent(1, st, c)

        loop(8, units)

    return progress, finish_all, wait_sent


def attention_role(s, rs, enter):
    nb, g, dcT = s.A.at[0], s.A.at[1], s.A.at[2]
    dn, S1 = s.ACC.at[0], s.ACC.at[1]

    def weights(gr, slot):
        return [
            pltpu.make_async_copy(
                s.w_qkv.at[:, at_multiple(j * 1024 + gr * 256, 256)], s.WA.at[slot, :, pl.ds(256 * j, 256)], s.qsem.at[slot, j]
            )
            for j in range(3)
        ]

    hc, gc = load_inputs(s)
    for cp in weights(0, 0):
        cp.start()
    dc = pltpu.make_async_copy(s.w_dense, s.WB, s.lsem.at[1, 0])
    dc.start()
    place = lax.broadcasted_iota(jnp.int32, (8, SEQ), 1)
    start = jnp.zeros((8, SEQ), jnp.int32)
    end = jnp.int32(0)
    for d in range(DOCS - 1):
        end = end + s.lens[0, d]
        start = jnp.where(place >= end, end, start)
    inv = np.float32(10000.0) ** (-(np.arange(0, ROT, 2, dtype=np.float32) / np.float32(ROT)))
    row = lax.broadcasted_iota(jnp.int32, (8, SEQ), 0)
    freq = jnp.zeros((8, SEQ), F32)
    for j in range(8):
        freq = jnp.where(row == j, float(inv[j]), freq)
    ang = (place - start).astype(F32) * freq
    co, si = jnp.cos(ang), jnp.sin(ang)
    one, zero = jnp.ones((48, SEQ), F32), jnp.zeros((48, SEQ), F32)
    for j, parts in enumerate(([co, co, one, co, co, one], [-si, si, zero, -si, si, zero])):
        table = jnp.concatenate(parts, axis=0).T
        for i in range(4):
            S1[768:1024, 256 * i + 128 * j : 256 * i + 128 * j + 128] = table[256 * i : 256 * i + 256]
    blocks = [(qb, kb) for qb in range(4) for kb in range(max(0, qb - 2), qb + 1)]

    def mask_at(qb, kb):
        n = blocks.index((qb, kb))
        return s.GO.at[8 + n // 4, :, pl.ds(256 * (n % 4), 256)]

    for qb, kb in blocks:
        kidx = lax.broadcasted_iota(jnp.int32, (256, 256), 0) + 256 * kb
        qidx = lax.broadcasted_iota(jnp.int32, (256, 256), 1) + 256 * qb
        st = start[0:1, 256 * qb : 256 * qb + 256]
        mask_at(qb, kb)[...] = jnp.where((kidx >= st) & (kidx <= qidx), 0.0, -1e9).astype(BF)
    for cp in hc:
        cp.wait()
    scoped('norm', layer_norm)(staged_rows(s), s.gain[...], s.shift[...], nb)
    gc.wait()
    dc.wait()
    s.bsum[...] = jnp.zeros((8, D), F32)

    def d_context(i):
        at = at_multiple(i * 512, 512)
        for q in range(4):
            dcT[pl.ds(256 * q, 256), at] = dot_t(s.WB[pl.ds(256 * q, 256), :], g[at, :]).astype(BF)
        s.bsum[...] += jnp.sum(g[at, :].astype(F32).reshape(64, 8, D), axis=0)
        dn[at, :] = jnp.zeros((512, D), F32)

    scoped('dctx', loop)(2, d_context)
    enter()
    E = lambda qb, n: s.GO.at[n + 3 * (qb % 2)]
    DS = lambda n: s.GO.at[11 + n]
    kT, vT = s.GO.at[6], s.GO.at[7]
    query, key, value, d_query = (s.RO2.at[n, :, pl.ds(256 * k, 256)] for n in range(2) for k in range(2))
    ones = jnp.ones((16, SEQ), BF)
    lane = lax.broadcasted_iota(jnp.int32, (256, 256), 1)

    def turn(x, i, sign):
        cosines, sines = (S1[768:1024, at_multiple(256 * i + 128 * j, 128)] for j in range(2))
        low = lax.broadcasted_iota(jnp.int32, (256, 128), 1) % 64 < 8
        parts = []
        for j in range(x.shape[1] // 128):
            u = x[:, 128 * j : 128 * j + 128]
            a = jnp.where(low, pltpu.roll(u, 120, 1), pltpu.roll(u, 8, 1)) * sines
            parts.append(u * cosines + a if sign > 0 else u * cosines - a)
        return jnp.concatenate(parts, axis=1)

    def stack(x):
        zb = jnp.zeros_like(x)
        return jnp.concatenate([jnp.where((lane >= 64 * h) & (lane < 64 * h + 64), x, zb) for h in range(4)], axis=0)

    def diag(x):
        return jnp.concatenate([x[64 * h : 64 * h + 64, 256 * h : 256 * h + 256] for h in range(4)], axis=0)

    def rows4(x):
        return jnp.concatenate([jnp.broadcast_to(x[:, 256 * h : 256 * h + 256], (64, 256)) for h in range(4)], axis=0)

    def sum4(x):
        return jnp.concatenate([jnp.sum(x[64 * h : 64 * h + 64], axis=0, keepdims=True) for h in range(4)], axis=1)

    def finish(gr, st):
        @pl.when(gr >= 0)
        def _():
            for j, order in enumerate(QKV_ORDERS):
                at = 1024 * j + 256 * gr
                rs.w_finish(order, st, 3 * gr + j, (at, at + 128))

    def group(gr):
        slot = lax.rem(gr, 2)

        @pl.when(gr < 3)
        def _():
            for cp in weights(gr + 1, 1 - slot):
                cp.start()

        for cp in weights(gr, slot):
            cp.wait()
        w = s.WA.at[slot]
        bq = jnp.concatenate([s.b_qkv[:, at_multiple(1024 * j + gr * 256, 256)] for j in range(3)], axis=1)

        with jax.named_scope("project"):
            for i in range(4):
                at = pl.ds(256 * i, 256)
                raw = dot(nb[at, :], w[...]) + bq
                query[at, :] = turn(raw[:, 0:256], i, 1).astype(BF) * BF(0.125)
                turned = turn(raw[:, 256:512], i, 1)
                key[at, :] = turned.astype(BF)
                kT[:, at] = turned.T.astype(BF)
                value[at, :] = raw[:, 512:768].astype(BF)
                vT[:, at] = raw[:, 512:768].T.astype(BF)
        crow = at_multiple(gr * 256, 256)
        s.PD[...] = jnp.zeros((SEQ, 512), F32)

        def keys_of(qb):
            return list(range(max(0, qb - 2), qb + 1))

        def score(qb, n, kb, q4):
            b = mask_at(qb, kb)[...].astype(F32)
            sc = dot_t(key[pl.ds(256 * kb, 256), :], q4) + jnp.concatenate([b] * 4, axis=1)
            S1[pl.ds(256 * n, 256), :] = sc
            return jnp.max(sc, axis=0, keepdims=True)

        def weigh(qb, n, m):
            E(qb, n)[...] = jnp.exp(S1[pl.ds(256 * n, 256), :] - m).astype(BF)

        def context(qb):
            kbs = keys_of(qb)
            nk = len(kbs)
            win, qs = pl.ds(256 * kbs[0], 256 * nk), pl.ds(256 * qb, 256)
            ev = s.GO[3 * (qb % 2) : 3 * (qb % 2) + nk].reshape(256 * nk, D)
            cx = dot(jnp.concatenate([vT[:, win], ones[:, 0 : 256 * nk]], axis=0), ev)
            li = 1.0 / cx[256:257, :]
            lsel = rows4(li)
            cT = diag(cx) * lsel
            dcs = (dcT[crow, qs].astype(F32) * lsel).astype(BF).astype(F32)
            dcT[crow, qs] = cT.astype(BF)
            return sum4(cT * dcs), stack(dcs.T.astype(BF))

        def back(qb, n, kb, q4, inner, dst):
            ks = pl.ds(256 * kb, 256)
            dP = dot_t(value[ks, :], dst)
            DS(n)[...] = (E(qb, n)[...].astype(F32) * (dP - inner)).astype(BF)
            s.PD[ks, 256:512] += dot(E(qb, n)[...], dst)
            s.PD[ks, 0:256] += dot(DS(n)[...], q4)

        def back_queries(qb):
            kbs = keys_of(qb)
            nk = len(kbs)
            dq = diag(dot(kT[:, pl.ds(256 * kbs[0], 256 * nk)], s.GO[11 : 11 + nk].reshape(256 * nk, D)))
            d_query[pl.ds(256 * qb, 256), :] = turn(dq.T * 0.125, qb, -1).astype(BF)

        with jax.named_scope("heads"):
            q4 = stack(query[0:256, :])
            m = score(0, 0, 0, q4)
            weigh(0, 0, m)
            inner, dst = context(0)
            for qb in range(4):
                kbs, after = keys_of(qb), keys_of(qb + 1) if qb < 3 else []
                q4_after = stack(query[256 * qb + 256 : 256 * qb + 512, :]) if after else None
                m = None
                for n in range(max(len(kbs), len(after))):
                    if n < len(after):
                        top = score(qb + 1, n, after[n], q4_after)
                        m = top if m is None else jnp.maximum(m, top)
                    if n < len(kbs):
                        back(qb, n, kbs[n], q4, inner, dst)
                for n in range(len(after)):
                    weigh(qb + 1, n, m)
                back_queries(qb)
                if after:
                    inner, dst = context(qb + 1)
                q4 = q4_after
        scoped('reduce', finish)(gr - 2, 1)
        for i in range(4):
            at = pl.ds(256 * i, 256)
            s.RO3[at, 0:256] = turn(s.PD[at, 0:256], i, -1).astype(BF)
        s.RO3[:, 256:512] = s.PD[:, 256:512].astype(BF)
        for q in range(4):
            tile = t_dot(nb[:, pl.ds(256 * q, 256)], jnp.concatenate([d_query[...], s.RO3[...]], axis=1)).astype(BF)
            for j in range(3):
                s.GW[3 * gr + j, q // 2, q % 2] = tile[:, 256 * j : 256 * j + 256].reshape(2, 2, 64, 256)
        for j, order in enumerate(QKV_ORDERS):
            rs.w_copy(order, 0, 3 * gr + j).start()
        for j in range(3):
            s.bcol[:, at_multiple(1024 * j + gr * 256, 256)] = jnp.sum(
                (d_query[...] if j == 0 else s.RO3[:, 256 * j - 256 : 256 * j]).astype(F32).reshape(128, 8, 256), axis=0
            )

        with jax.named_scope("dnormed"):
            for i in range(4):
                at = pl.ds(256 * i, 256)
                dn[at, :] += dot_t(jnp.concatenate([d_query[at, :], s.RO3[at, :]], axis=1), w[...])
        scoped('reduce', finish)(gr - 2, 2)
        scoped('reduce', finish)(gr - 1, 0)

    loop(4, scoped('group', group))

    for q in range(4):
        tile = dot(dcT[pl.ds(256 * q, 256), :], g[...]).astype(BF)
        for j in range(4):
            s.GW[12 + j, q // 2, q % 2] = tile[:, 256 * j : 256 * j + 256].reshape(2, 2, 64, 256)
    for j in range(4):
        rs.w_copy(DENSE_ORDERS[j], 0, 12 + j).start()

    for i in range(4):
        at = pl.ds(256 * i, 256)
        S1[at, :] = t_dot(dcT[:, at], s.WB[...])
    for j in range(3):
        s.VEC[j : j + 1, :] = jnp.sum(s.bcol[:, 1024 * j : 1024 * j + 1024], axis=0, keepdims=True)
    s.VEC[3:4, :] = jnp.sum(s.bsum[...], axis=0, keepdims=True)
    s.VEC[6:8, :] = jnp.zeros((2, D), F32)

    def progress(t):
        if t == 7:
            finish(2, 1)
        if t == 9:
            finish(2, 2)
        if 8 <= t < 11:
            finish(3, t - 8)
            for j in range(4):
                rs.w_finish(DENSE_ORDERS[j], t - 8, 12 + j, None)

    def finish_all():
        def units(gr):
            finish(gr, 3)

        loop(4, units)
        for j in range(4):
            rs.w_finish(DENSE_ORDERS[j], 3, 12 + j, (3072 + 256 * j, 3200 + 256 * j))

    def wait_sent():
        def units(gr):
            for st in range(4):
                for j, order in enumerate(QKV_ORDERS):
                    rs.w_copy(order, st, 3 * gr + j).wait_send()

        loop(4, units)
        for j in range(4):
            for st in range(4):
                rs.w_copy(DENSE_ORDERS[j], st, 12 + j).wait_send()

    return progress, finish_all, wait_sent


def kernel(extra, *refs):
    s = Scope()
    names = INPUTS + OUTPUTS + tuple(n for n, *_ in SCRATCH) + tuple(n for n, *_ in SEMS) + ("ready",)
    for n, r in zip(names, refs, strict=True):
        setattr(s, n, r)
    rs = Reducer(s, extra)
    pr, dp = rs.pr, rs.dp
    other = (dp, 1 - pr)
    barrier = pltpu.get_barrier_semaphore()
    for b in range(4):
        pl.semaphore_signal(barrier, inc=1, device_id=(rs.partner[b], pr), device_id_type=MESH)
    for line in rs.lines:
        pl.semaphore_signal(barrier, inc=1, device_id=(line[2], pr), device_id_type=MESH)
    pl.semaphore_signal(barrier, inc=1, device_id=other, device_id_type=MESH)
    enter = lambda: pl.semaphore_wait(barrier, 7)

    def to_other(src, dst, ss, sr):
        return pltpu.make_async_remote_copy(src_ref=src, dst_ref=dst, send_sem=ss, recv_sem=sr, device_id=other, device_id_type=MESH)

    def role(is_attention, run, bias):
        progress, finish_all, wait_sent = run(s, rs, enter)
        own_half = 0 if is_attention else 1
        mine, theirs = pl.ds(512 * own_half, 512), pl.ds(512 * (1 - own_half), 512)
        if not is_attention:
            pl.semaphore_signal(s.ready, inc=1, device_id=other, device_id_type=MESH)
        hc = pltpu.make_async_copy(s.hidden, s.A.at[2], s.hsem.at[5])
        hc.start()
        branch = s.A.at[0]

        def pack(i):
            at = at_multiple(i * 128, 128)
            branch[at, :] = (s.ACC[1, at, :] + bias[...]).astype(BF)
            s.WB[at, :] = s.ACC[0, at, :].astype(BF)

        scoped('pack', loop)(8, pack)
        if is_attention:
            pl.semaphore_wait(s.ready, 1)
        to_feed = (s.WA.at[1, pl.ds(0, 512), pl.ds(256, 512)], s.WA.at[1, pl.ds(512, 512), pl.ds(256, 512)], s.WA.at[0], s.WA.at[1, :, pl.ds(0, 256)])
        to_attention = tuple(s.RO1.at[n // 16, n // 2 % 8, n % 2] for n in range(24))
        give_feed = (branch.at[theirs, pl.ds(0, 512)], branch.at[theirs, pl.ds(512, 512)], s.WB.at[:, pl.ds(0, 768)], s.WB.at[:, pl.ds(768, 256)])
        give_attention = tuple(s.WB.at[pl.ds(128 * (n // 2), 128), pl.ds(512 * (n % 2), 512)] for n in range(16)) + tuple(
            branch.at[pl.ds(512 * (1 - own_half) + 128 * (n // 2), 128), pl.ds(512 * (n % 2), 512)] for n in range(8)
        )
        give, land = (give_feed, to_feed) if is_attention else (give_attention, to_attention)
        moves = [to_other(src, dst, s.xs.at[n], s.xr.at[n]) for n, (src, dst) in enumerate(zip(give, land))]
        for cp in moves:
            cp.start()
        def start_vectors(hop):
            copies = [
                pltpu.make_async_remote_copy(
                    src_ref=s.VEC, dst_ref=s.VRECV.at[3 * hop + k], send_sem=s.vs.at[3 * hop + k], recv_sem=s.vr.at[3 * hop + k],
                    device_id=(to, pr), device_id_type=MESH,
                )
                for k, to in enumerate(rs.lines[hop])
            ]
            for cp in copies:
                cp.start()
            return copies

        def end_vectors(hop, copies):
            for cp in copies:
                scoped('vec', cp.wait)()
            s.VEC[...] += s.VRECV[3 * hop] + s.VRECV[3 * hop + 1] + s.VRECV[3 * hop + 2]

        if not is_attention:
            copies = start_vectors(0)
            for t in range(8, 8 + LAGS[2]):
                scoped(f'reduce{t}', progress)(t)
                if t == 9:
                    end_vectors(0, copies)
                    copies = start_vectors(1)
            end_vectors(1, copies)
        else:
            progress(7)
        hc.wait()
        give, land = (give_attention, to_attention) if is_attention else (give_feed, to_feed)
        for n, (src, dst) in enumerate(zip(give, land)):
            scoped('moves', to_other(src, dst, s.xs.at[n], s.xr.at[n]).wait_recv)()
        s.lnsum[...] = jnp.zeros((2, 8, D), F32)

        def last(i):
            at = at_multiple(i * 128, 128)
            x = s.A[2, at, :].astype(F32)
            mean = jnp.mean(x, axis=1, keepdims=True)
            cen = x - mean
            inv = lax.rsqrt(jnp.mean(cen * cen, axis=1, keepdims=True) + EPS)
            x_hat = cen * inv
            a = s.WB[at, :].astype(F32)
            if is_attention:
                b = jnp.concatenate([s.RO1[0, i, n] for n in range(2)], axis=1).astype(F32)
            else:
                b = jnp.concatenate([s.WA[0, at, :], s.WA[1, at, 0:256]], axis=1).astype(F32)
            dnv = (a + b).astype(BF).astype(F32)
            e = dnv * s.gain[...]
            grad = s.A[1, at, :].astype(F32) + inv * (
                e - jnp.mean(e, axis=1, keepdims=True) - x_hat * jnp.mean(e * x_hat, axis=1, keepdims=True)
            )
            if is_attention:
                s.lnsum[0] += jnp.sum((dnv * x_hat).reshape(16, 8, D), axis=0)
                s.lnsum[1] += jnp.sum(dnv.reshape(16, 8, D), axis=0)

            @pl.when(i // 4 == own_half)
            def _():
                if is_attention:
                    got = jnp.concatenate([s.RO1[1, lax.rem(i, 4), n] for n in range(2)], axis=1)
                else:
                    here = 128 * lax.rem(i, 4)
                    got = jnp.concatenate([s.WA[1, at_multiple(here, 128), 256:768], s.WA[1, at_multiple(512 + here, 128), 256:768]], axis=1)
                attn, mlp = (branch[at, :], got) if is_attention else (got, branch[at, :])
                branch[at, :] = (x + attn.astype(F32) + mlp.astype(F32)).astype(BF)

            s.A[2, at, :] = grad.astype(BF)

        scoped('last', loop)(8, last)
        outs = [
            pltpu.make_async_copy(branch.at[mine], s.o_out, s.fl.at[0]),
            pltpu.make_async_copy(s.A.at[2], s.o_ig, s.fl.at[1]),
        ]
        for cp in outs:
            cp.start()
        if is_attention:
            for j in range(2):
                s.VEC[4 + j : 5 + j, :] = jnp.sum(s.lnsum[j], axis=0, keepdims=True)
        if is_attention:
            for hop in range(2):
                copies = start_vectors(hop)
                scoped(f'reduce{8 + hop}', progress)(8 + hop)
                end_vectors(hop, copies)
        vx = to_other(s.VEC, s.VPART, s.vs.at[6], s.vr.at[6])
        vx.start()
        if is_attention:
            scoped('reduce10', progress)(10)
        scoped('finish', finish_all)()

        def split(first, size, half):
            return pl.ds(first, size) if extra > 1 else pl.ds(first + half * (size // 2), size // 2)

        def pieces(attention, half):
            wide = [s.o_qkv.at[:, pl.ds(1024 * k, 1024)] for k in range(3)] + [s.o_dense]
            if not attention:
                wide = [s.o_in.at[:, pl.ds(1024 * k, 1024)] for k in range(4)]
            parts = [(s.ACC.at[0, split(64 * k, 64, half)], to) for k, to in enumerate(wide)]
            return parts if attention else parts + [(s.ACC.at[0, split(256, 256, half)], s.o_outw)]

        sent, local = [], []
        for n, (src, dst) in enumerate(pieces(is_attention, 1 - own_half)):
            cp = to_other(src, dst, s.fs.at[n], s.fr.at[n])
            cp.start()
            sent.append(cp)
        for n, (src, dst) in enumerate(pieces(is_attention, own_half)):
            cp = pltpu.make_async_copy(src, dst, s.fl.at[2 + n])
            cp.start()
            local.append(cp)
        vx.wait()
        s.o_vec[0 if is_attention else 1] = s.VEC[...]
        s.o_vec[1 if is_attention else 0] = s.VPART[...]
        scoped('sent', wait_sent)()
        for cp in moves:
            cp.wait_send()
        for cp in outs + local:
            cp.wait()
        for cp in sent:
            cp.wait_send()
        for n, (src, dst) in enumerate(pieces(not is_attention, own_half)):
            to_other(src, dst, s.fs.at[n], s.fr.at[n]).wait_recv()

    pl.when(pr == 0)(lambda: role(True, attention_role, s.b_dense))
    pl.when(pr == 1)(lambda: role(False, feed_role, s.b_out))


def call(extra, *args):
    rows = 32 if extra == 1 else 64
    outw = 128 if extra == 1 else 256
    anywhere, vmem, smem = (pl.BlockSpec(memory_space=m) for m in (pl.ANY, pltpu.VMEM, pltpu.SMEM))
    shapes = [
        ((512, D), BF), ((SEQ, D), BF), ((rows, 3072), F32), ((rows, D), F32), ((rows, FF), F32), ((outw, D), F32), ((2, 8, D), F32),
    ]
    return pl.pallas_call(
        partial(kernel, extra),
        out_shape=[jax.ShapeDtypeStruct(*x) for x in shapes],
        in_specs=[anywhere, smem, vmem, vmem, anywhere, vmem, anywhere, vmem, anywhere, vmem, anywhere, vmem, anywhere],
        out_specs=[anywhere] * 6 + [vmem],
        scratch_shapes=[pltpu.VMEM(shape, kind) for _, shape, kind in SCRATCH]
        + [pltpu.SemaphoreType.DMA(shape) for _, shape in SEMS]
        + [pltpu.SemaphoreType.REGULAR],
        compiler_params=pltpu.CompilerParams(collective_id=0, has_side_effects=True, vmem_limit_bytes=VMEM_LIMIT),
        cost_estimate=pl.CostEstimate(flops=50 * 10**9, bytes_accessed=40 * 10**6, transcendentals=10**7),
    )(*args)


VMEM_LIMIT = 62 * 2**20


def deliver(count, *refs):
    big, vec, outs, small, held, sems = refs[:6], refs[6], refs[7:13], refs[13:19], refs[19:25], refs[25]
    take = [pltpu.make_async_copy(src, mid, sems.at[0, n]) for n, (src, mid) in enumerate(zip(big, held))]
    give = [pltpu.make_async_copy(mid, dst, sems.at[1, n]) for n, (mid, dst) in enumerate(zip(held, outs))]
    for cp in take:
        cp.start()
    place = lax.axis_index("dp") * 2 + lax.axis_index("pair")

    def tile(role, row, at):
        held = vec[role, :, at_multiple(128 * lax.rem(at, 8), 128)]
        return jnp.sum(jnp.where(sub == row + at // 8, held, 0.0), axis=0, keepdims=True)

    lane = lax.broadcasted_iota(jnp.int32, (1, 128), 1)
    sub = lax.broadcasted_iota(jnp.int32, (8, 128), 0)
    for out, (role, row, rows) in zip(small, ((0, 0, 3), (0, 3, 1), (1, 0, 4), (1, 4, 1), (0, 4, 1), (0, 5, 1))):
        size = rows * D // count
        at = place * size
        first, skip = at // 128, lax.rem(at, 128)
        turned = pltpu.roll(tile(role, row, first), lax.rem(128 - skip, 128), 1)
        if 128 % size:
            after = pltpu.roll(tile(role, row, jnp.minimum(first + 1, 8 * rows - 1)), lax.rem(128 - skip, 128), 1)
            turned = jnp.where(lane < 128 - skip, turned, after)
        out[...] = turned[:, 0:size]
    for one, other in zip(take, give):
        one.wait()
        other.start()
    for cp in give:
        cp.wait()


def swap(x, bit):
    return lax.ppermute(x, "dp", [(i, i ^ bit) for i in range(lax.axis_size("dp"))])


def halve(x, bit):
    half = x.shape[0] // 2
    up = (lax.axis_index("dp") // bit) % 2
    keep = lax.dynamic_slice_in_dim(x, up * half, half, 0)
    give = lax.dynamic_slice_in_dim(x, (1 - up) * half, half, 0)
    return keep + swap(give, bit)


def body(hidden, doc_lengths, ln_gain, ln_bias, qkv_weight, qkv_bias, dense_weight, dense_bias, fc_in_weight, fc_in_bias, fc_out_weight, fc_out_bias, cotangent):
    extra = lax.axis_size("dp") // INNER
    output, input_grad, qkv, dense, w_in, w_out, vec = call(
        extra, hidden, doc_lengths, ln_gain[None], ln_bias[None], qkv_weight, qkv_bias[None], dense_weight, dense_bias[None],
        fc_in_weight, fc_in_bias[None], fc_out_weight, fc_out_bias[None], cotangent,
    )
    dp, pair = lax.axis_index("dp"), lax.axis_index("pair")
    if extra > 1:
        bit = extra // 2
        while bit:
            qkv, dense, w_in, w_out = (halve(x, bit) for x in (qkv, dense, w_in, w_out))
            vec = vec + swap(vec, bit)
            bit //= 2
        qkv, dense, w_in, w_out = (
            lax.dynamic_slice_in_dim(x, pair * (x.shape[0] // 2), x.shape[0] // 2, 0) for x in (qkv, dense, w_in, w_out)
        )
    big = (output, input_grad, qkv, dense, w_in, w_out)
    count = lax.axis_size("dp") * 2
    sizes = (3072, D, FF, D, D, D)
    *big, qkv_b, dense_b, in_b, out_b, gain, shift = pl.pallas_call(
        partial(deliver, count),
        out_shape=[jax.ShapeDtypeStruct(x.shape, x.dtype) for x in big]
        + [jax.ShapeDtypeStruct((1, n // count), F32) for n in sizes],
        in_specs=[pl.BlockSpec(memory_space=pl.ANY)] * 6 + [pl.BlockSpec(memory_space=pltpu.VMEM)],
        out_specs=[pl.BlockSpec(memory_space=pl.ANY)] * 6 + [pl.BlockSpec(memory_space=pltpu.VMEM)] * 6,
        scratch_shapes=[pltpu.VMEM(x.shape, x.dtype) for x in big] + [pltpu.SemaphoreType.DMA((2, 6))],
    )(*big, vec)
    output, input_grad, qkv, dense, w_in, w_out = big
    qkv_b, dense_b, in_b, out_b, gain, shift = (x.reshape(-1) for x in (qkv_b, dense_b, in_b, out_b, gain, shift))
    return output, input_grad, qkv, qkv_b, dense, dense_b, w_in, in_b, w_out, out_b, gain, shift


def solution(mesh):
    rows = P("dp", None)
    shard, shard1 = P(("dp", "pair"), None), P(("dp", "pair"))
    return jax.shard_map(
        body,
        mesh=mesh,
        in_specs=(rows, rows) + (P(),) * 10 + (rows,),
        out_specs=(shard, rows, shard, shard1, shard, shard1, shard, shard1, shard, shard1, shard1, shard1),
        check_vma=False,
    )
```

time: 185 us -> 132 us (0.71)
  Pallas kernels: 171 us -> 131 us
  local copies, waits for them, and re-layouts: 11.5 us -> 0 us
    pallas_call x1, Pallas kernels: 171 us -> 126 us  [call(): pl.pallas_call(partial(kernel, extra), out_shape=[jax.ShapeDtypeStruct(*x...]
    unnamed x18 -> x0, local copies, waits for them, and re-layouts: 7.5 us -> none
    pallas_call x0 -> x1, Pallas kernels: none -> 5.26 us  [body(): pl.pallas_call(partial(deliver, count), out_shape=[jax.ShapeDtypeStruct(x...]
    dynamic_slice x4 -> x0, local copies, waits for them, and re-layouts: 2.34 us -> none  [own(): return lax.dynamic_slice_in_dim(x, place * size, size, 0)]
where the time goes in v2:
time: 132 us
  Pallas kernels  131 us (99%)
    pallas_call x1, Pallas kernels, call(): pl.pallas_call(partial(kernel, extra), out_shape=[jax.ShapeDtypeStruct(*x...  126 us
    pallas_call x1, Pallas kernels, body(): pl.pallas_call(partial(deliver, count), out_shape=[jax.ShapeDtypeStruct(x...  5.26 us

profile of v2, /device:TPU:3, one launch (start us, length us, event | category | flops | bytes accessed | tf_op | source)
XLA Modules:
  0.0 131.8 jit_solution(1065428893760994633)
XLA Ops:
  0.6 125.7 %shard_map.220 = (bf16[512,1024]{1,0:T(8,128)(2,1)}, bf16[1024,1024]{1,0:T(8,128)(2,1)}, f32[32,3072]{1,0:T(8,128)}, f32[32,1024]{1,0:T(8,128)}, f32[32,4096]{1,...) custom-call(bf16[1024,1024]{1,0:T(8,128)(2,1)} %refs_0_.1, s32[1,8]{1,0:T(1,128)} %refs_1_.1, f32[1,1024]{1,0:T(1,128)} %bitcast.14, ...), custom_call_target="tpu_custom_call" | custom-call | flops 49999998976 | bytes 40000000 | tf_op jit(solution)/shard_map/pallas_call | solution.py:822
  126.3 5.3 %shard_map.221 = (bf16[512,1024]{1,0:T(8,128)(2,1)}, bf16[1024,1024]{1,0:T(8,128)(2,1)}, f32[32,3072]{1,0:T(8,128)}, f32[32,1024]{1,0:T(8,128)}, f32[32,4096]{1,...) custom-call(bf16[512,1024]{1,0:T(8,128)(2,1)} %get-tuple-element.31., ...), custom_call_target="tpu_custom_call" | custom-call | tf_op jit(solution)/shard_map/pallas_call | solution.py:899

commit v3 on v2

--- a/solution.py
+++ b/solution.py
@@ -13,11 +13,9 @@
 EPS = 1e-05
 SEQ, D, FF, HEAD, ROT, DOCS = 1024, 1024, 4096, 64, 16, 8
 INNER = 16
-X_FIRST, Y_FIRST, Z_FIRST, X_THEN_Z = (0, 1, 2, 3), (1, 0, 2, 3), (2, 1, 0, 3), (0, 2, 1, 3)
-W_ORDERS = (X_FIRST, Y_FIRST)
-O_ORDERS = (Z_FIRST, X_THEN_Z)
-QKV_ORDERS = (X_FIRST, Y_FIRST, Z_FIRST)
-DENSE_ORDERS = (Y_FIRST, Y_FIRST, Z_FIRST, X_FIRST)
+W_ORDERS = ((1, 0, 2, 3), (0, 1, 2, 3))
+O_ORDERS = ((1, 2, 0, 3), (2, 0, 1, 3))
+QKV_ORDERS = ((2, 1, 0, 3), (0, 1, 2, 3), (0, 2, 1, 3))
 LAGS = (1, 2, 3)
 
 
@@ -76,6 +74,10 @@
     ("RO2", (2, SEQ, 512), BF),
     ("RO3", (SEQ, 512), BF),
     ("RO4", (2, 2, 128, 512), BF),
+    ("gain", (1, D), F32),
+    ("shift", (1, D), F32),
+    ("b_first", (1, 4096), F32),
+    ("b_last", (1, D), F32),
     ("bcol", (8, 4096), F32),
     ("bsum", (8, D), F32),
     ("lnsum", (2, 8, D), F32),
@@ -84,22 +86,27 @@
     ("VPART", (8, D), F32),
 )
 SEMS = (
-    ("lsem", (2, 8)),
+    ("lsem", (2, 2)),
     ("hsem", (6,)),
-    ("qsem", (2, 3)),
-    ("ws", (16, 4)),
-    ("wr", (16, 4)),
-    ("os", (2, 8, 5)),
-    ("orr", (2, 8, 5)),
+    ("qsem", (2,)),
+    ("ws", (4,)),
+    ("wr", (8, 4)),
+    ("os", (2, 4)),
+    ("orr", (8, 2)),
+    ("orr2", (2, 4)),
+    ("orr3", (2, 2)),
+    ("ds", (4,)),
+    ("dr", (4, 4)),
     ("vs", (7,)),
     ("vr", (7,)),
-    ("xs", (24,)),
-    ("xr", (24,)),
+    ("xs", (1,)),
+    ("xr", (1,)),
     ("fs", (5,)),
     ("fr", (5,)),
-    ("fl", (7,)),
+    ("fl", (9,)),
+    ("bsem", (4,)),
 )
-INPUTS = ("hidden", "lens", "gain", "shift", "w_qkv", "b_qkv", "w_dense", "b_dense", "w_in", "b_in", "w_out", "b_out", "cot")
+INPUTS = ("hidden", "lens", "h_gain", "h_shift", "w_qkv", "hb_qkv", "w_dense", "hb_dense", "w_in", "hb_in", "w_out", "hb_out", "cot")
 OUTPUTS = ("o_out", "o_ig", "o_qkv", "o_dense", "o_in", "o_outw", "o_vec")
 
 
@@ -119,31 +126,106 @@
             src_ref=src, dst_ref=dst, send_sem=ss, recv_sem=rs, device_id=(self.partner[b], self.pr), device_id_type=MESH
         )
 
+    def wait_bytes(self, ref, sem, sent):
+        cp = self.to(ref, ref, sem, sem, 0)
+        cp.wait_send() if sent else cp.wait_recv()
+
     def w_half(self, order, st, u, bit):
         s = self.s
         left = [b for b in (3, 2, 1, 0) if b not in order[:st]]
         ref = (s.GW, s.RW1, s.RW2, s.RW3)[st]
         return ref.at[(u,) + (slice(None),) * left.index(order[st]) + (bit,)]
 
-    def w_copy(self, order, st, u):
+    def w_copy(self, order, st, u, k):
         s, b = self.s, order[st]
         dst = (s.RW1, s.RW2, s.RW3, s.RW4)[st].at[u]
-        return self.to(self.w_half(order, st, u, 1 - self.bits[b]), dst, s.ws.at[u, st], s.wr.at[u, st], b)
-
-    def w_finish(self, order, st, u, cols):
+        return self.to(self.w_half(order, st, u, 1 - self.bits[b]), dst, s.ws.at[st], s.wr.at[k, st], b)
+
+    def w_wait(self, st, u, n, k):
+        s = self.s
+        self.wait_bytes((s.RW1, s.RW2, s.RW3, s.RW4)[st].at[pl.ds(u, n)], s.wr.at[k, st], False)
+
+    def w_wait_sent(self, n):
+        s = self.s
+        for st, ref in enumerate((s.RW1, s.RW2, s.RW3, s.RW4)):
+            self.wait_bytes(ref.at[pl.ds(0, n)], s.ws.at[st], True)
+
+    def w_finish(self, order, st, u, k, cols):
         s, b = self.s, order[st]
-        self.w_copy(order, st, u).wait_recv()
         kept = self.w_half(order, st, u, self.bits[b])
         got = (s.RW1, s.RW2, s.RW3, s.RW4)[st].at[u]
         if st < 3:
             lead = got.shape[0]
             for i in range(lead):
                 got[i] = (got[i].astype(F32) + kept[i].astype(F32)).astype(BF)
-            self.w_copy(order, st + 1, u).start()
+            self.w_copy(order, st + 1, u, k).start()
         else:
             total = got[...].astype(F32) + kept[...].astype(F32)
             for i, at in enumerate(cols):
                 s.ACC[0, at_multiple(64 * (at // 1024), 64), at_multiple(lax.rem(at, 1024), 128)] = total[:, 128 * i : 128 * i + 128]
+
+    def d_copies(self, st, gr):
+        s, (x, y, zl, zh) = self.s, self.bits
+        u = 12 + gr
+        low, high = zl == gr % 2, zh == gr // 2
+
+        def copy(src, dst, bit):
+            return self.to(src, dst, s.ds.at[st], s.dr.at[gr, st], bit)
+
+        if st == 0:
+            return True, True, [
+                copy(s.GW.at[u, 0, :, :, 1 - x], s.RW1.at[u, 0], 0), copy(s.GW.at[u, 1, :, 1 - y], s.RW1.at[u, 1], 1)
+            ]
+        if st == 1:
+            return True, True, [
+                copy(s.RW1.at[u, 0, :, 1 - y], s.RW2.at[u, 0], 1), copy(s.RW1.at[u, 1, :, 1 - x], s.RW2.at[u, 1], 0)
+            ]
+        if st == 2:
+            return jnp.logical_not(low), low, [copy(s.RW2.at[u], self.d3(gr), 2)]
+        return low & jnp.logical_not(high), low & high, [copy(self.d3(gr).at[j], s.RW4.at[pl.ds(12 + 2 * j, 2)], 3) for j in range(2)]
+
+    def d3(self, gr):
+        return self.s.RW3.at[pl.ds(12 + 2 * (gr // 2), 2)]
+
+    def d_start(self, st, gr):
+        sends, _, copies = self.d_copies(st, gr)
+
+        @pl.when(sends)
+        def _():
+            for cp in copies:
+                cp.start()
+
+    def d_wait_sent(self):
+        s, (x, y, zl, zh) = self.s, self.bits
+        units = pl.ds(12, 4)
+        for st, ref in enumerate((s.RW1.at[units], s.RW2.at[units], s.RW3.at[units], s.RW4.at[units])):
+            self.wait_bytes(ref, s.ds.at[st], True)
+
+    def d_finish(self, st, gr):
+        s, (x, y, _, _) = self.s, self.bits
+        u = 12 + gr
+        _, takes, copies = self.d_copies(st, gr)
+
+        @pl.when(takes)
+        def _():
+            self.wait_bytes((s.RW1.at[u], s.RW2.at[u], self.d3(gr), s.RW4.at[pl.ds(12, 4)])[st], s.dr.at[gr, st], False)
+            if st == 0:
+                for j in range(2):
+                    s.RW1[u, 0, j] = (s.RW1[u, 0, j].astype(F32) + s.GW[u, 0, j, :, x].astype(F32)).astype(BF)
+                    s.RW1[u, 1, j] = (s.RW1[u, 1, j].astype(F32) + s.GW[u, 1, j, y].astype(F32)).astype(BF)
+            elif st == 1:
+                s.RW2[u, 0] = (s.RW2[u, 0].astype(F32) + s.RW1[u, 0, :, y].astype(F32)).astype(BF)
+                s.RW2[u, 1] = (s.RW2[u, 1].astype(F32) + s.RW1[u, 1, :, x].astype(F32)).astype(BF)
+            elif st == 2:
+                got = self.d3(gr)
+                got[...] = (got[...].astype(F32) + s.RW2[u].astype(F32)).astype(BF)
+            else:
+                for j in range(4):
+                    total = s.RW4[12 + j].astype(F32) + self.d3(gr)[j // 2, j % 2].astype(F32)
+                    s.ACC[0, 192:256, 256 * j : 256 * j + 256] = total
+
+        if st < 3:
+            self.d_start(st + 1, gr)
 
     def chunk_of(self, c):
         return c % 2, (c // 2) % 2, c // 4
@@ -171,20 +253,21 @@
         here = xor(a, xor(own[p], own[q])) == own[r]
         mine = here & (xor(b, own[0]) == own[3])
 
-        def copy(src, dst, k, bit):
-            return self.to(src, dst, s.os.at[n, c, k], s.orr.at[n, c, k], bit)
+        def copy(src, dst, bit):
+            come = s.orr.at[c, st] if st < 2 else s.orr2.at[n, c // 2] if st == 2 else s.orr3.at[n, h]
+            return self.to(src, dst, s.os.at[n, st], come, bit)
 
         if st == 0:
             copies = []
             for k in range(2):
                 src = s.GO.at[self.o_shard(n, c, 1 - own[p], k), at_multiple(128 * h, 128), pl.ds(512 * n, 512)]
-                copies.append(copy(src, s.RO1.at[n, c, k], k, p))
+                copies.append(copy(src, s.RO1.at[n, c, k], p))
             return True, True, copies
         if st == 1:
-            return True, True, [copy(s.RO1.at[n, c, 1 - own[q]], self.ro2(n, c), 2, q)]
+            return True, True, [copy(s.RO1.at[n, c, 1 - own[q]], self.ro2(n, c), q)]
         if st == 2:
-            return jnp.logical_not(here), here, [copy(self.ro2(n, c), self.ro3(n, c), 3, r)]
-        return here & jnp.logical_not(mine), mine, [copy(self.ro3(n, c), s.RO4.at[n, h], 4, 3)]
+            return jnp.logical_not(here), here, [copy(self.ro2(n, c), self.ro3(n, c), r)]
+        return here & jnp.logical_not(mine), mine, [copy(self.ro3(n, c), s.RO4.at[n, h], 3)]
 
     def o_start(self, n, st, c):
         sends, _, copies = self.o_copies(n, st, c)
@@ -194,13 +277,15 @@
             for cp in copies:
                 cp.start()
 
-    def o_wait_sent(self, n, st, c):
-        sends, _, copies = self.o_copies(n, st, c)
-
-        @pl.when(sends)
-        def _():
-            for cp in copies:
-                cp.wait_send()
+    def o_wait_sent(self):
+        s = self.s
+        for n in range(2):
+            for st, ref in enumerate((s.RO1.at[n], s.RO2.at[n], s.RO3.at[pl.ds(512 * n, 512)], s.RO4.at[n])):
+                self.wait_bytes(ref, s.os.at[n, st], True)
+
+    def o_wait(self, st, c):
+        s = self.s
+        self.wait_bytes(s.RO1.at[:, c] if st == 0 else s.RO2.at[:, at_multiple(128 * c, 128)], s.orr.at[c, st], False)
 
     def o_finish(self, n, st, c):
         s, own = self.s, self.bits
@@ -211,8 +296,8 @@
 
         @pl.when(takes)
         def _():
-            for cp in copies:
-                cp.wait_recv()
+            if st > 1:
+                copies[0].wait_recv()
             if st == 0:
                 for k in range(2):
                     kept = s.GO[self.o_shard(n, c, own[p], k), at_multiple(128 * h, 128), lanes]
@@ -230,15 +315,12 @@
             self.o_start(n, st + 1, c)
 
 
-def layer_norm(load_rows, gain, shift, nb):
-    def tile(i):
-        x = load_rows(i).astype(F32)
-        mean = jnp.mean(x, axis=1, keepdims=True)
-        cen = x - mean
-        inv = lax.rsqrt(jnp.mean(cen * cen, axis=1, keepdims=True) + EPS)
-        nb[at_multiple(i * 128, 128), :] = (cen * inv * gain + shift).astype(BF)
-
-    loop(8, tile)
+def layer_norm(x, gain, shift):
+    x = x.astype(F32)
+    mean = jnp.mean(x, axis=1, keepdims=True)
+    cen = x - mean
+    inv = lax.rsqrt(jnp.mean(cen * cen, axis=1, keepdims=True) + EPS)
+    return (cen * inv * gain + shift).astype(BF)
 
 
 A1, A2, A3, A4, A5 = 0.254829592, -0.284496736, 1.421413741, -1.453152027, 1.061405429
@@ -253,17 +335,28 @@
     return cdf, x * (e * 0.3989422804014327)
 
 
-def load_inputs(s):
+def load_inputs(s, first, last):
     hc = [pltpu.make_async_copy(s.hidden.at[pl.ds(256 * j, 256)], s.GO.at[12 + j], s.hsem.at[j]) for j in range(4)]
     gc = pltpu.make_async_copy(s.cot, s.A.at[1], s.hsem.at[4])
-    for cp in hc:
+    n = first.shape[1]
+    vectors = ((s.h_gain, s.gain), (s.h_shift, s.shift), (first, s.b_first.at[:, pl.ds(0, n)]), (last, s.b_last))
+    vc = [pltpu.make_async_copy(src, dst, s.bsem.at[j]) for j, (src, dst) in enumerate(vectors)]
+    for cp in hc + vc:
         cp.start()
-    gc.start()
-    return hc, gc
-
-
-def staged_rows(s):
-    return lambda i: s.GO[12 + i // 2, at_multiple(128 * lax.rem(i, 2), 128), :]
+    return hc, vc, gc
+
+
+def column_sums(s):
+    def tile(i):
+        s.bsum[...] += jnp.sum(s.A[1, at_multiple(i * 256, 256), :].astype(F32).reshape(32, 8, D), axis=0)
+
+    s.bsum[...] = jnp.zeros((8, D), F32)
+    loop(4, tile)
+    return jnp.sum(s.bsum[...], axis=0, keepdims=True)
+
+
+def staged_rows(s, i):
+    return s.GO[12 + i // 2, at_multiple(128 * lax.rem(i, 2), 128), :]
 
 
 def feed_role(s, rs, enter):
@@ -277,27 +370,34 @@
     def weights(c, slot):
         copies = []
         for p, at in enumerate(units_at(c)):
-            cols, k = at_multiple(at, 128), 4 * slot + p
-            copies.append(pltpu.make_async_copy(s.w_in.at[:, cols], s.WA.at[slot, :, pl.ds(128 * p, 128)], s.lsem.at[0, k]))
-            copies.append(pltpu.make_async_copy(s.w_out.at[cols, :], s.WB.at[at_multiple(512 * slot + 128 * p, 128)], s.lsem.at[1, k]))
+            cols = at_multiple(at, 128)
+            copies.append(pltpu.make_async_copy(s.w_in.at[:, cols], s.WA.at[slot, :, pl.ds(128 * p, 128)], s.lsem.at[0, slot]))
+            copies.append(pltpu.make_async_copy(s.w_out.at[cols, :], s.WB.at[at_multiple(512 * slot + 128 * p, 128)], s.lsem.at[1, slot]))
         return copies
 
-    hc, gc = load_inputs(s)
-    for cp in weights(0, 0):
-        cp.start()
-    for cp in hc:
+    def weights_here(slot):
+        pltpu.make_async_copy(s.w_in.at[:, pl.ds(0, 512)], s.WA.at[slot, :, pl.ds(0, 512)], s.lsem.at[0, slot]).wait()
+        pltpu.make_async_copy(s.w_out.at[pl.ds(0, 512), :], s.WB.at[at_multiple(512 * slot, 512)], s.lsem.at[1, slot]).wait()
+
+    hc, vc, gc = load_inputs(s, s.hb_in, s.hb_out)
+    for cp in vc:
         cp.wait()
-    scoped('norm', layer_norm)(staged_rows(s), s.gain[...], s.shift[...], nb)
-    gc.wait()
-    s.bsum[...] = jnp.zeros((8, D), F32)
-
-    def prepare(i):
+
+    def norm(i):
         at = at_multiple(i * 128, 128)
-        s.bsum[...] += jnp.sum(g[at, :].astype(F32).reshape(16, 8, D), axis=0)
+        nb[at, :] = layer_norm(staged_rows(s, i), s.gain[...], s.shift[...])
         dn[at, :] = jnp.zeros((128, D), F32)
         out[at, :] = jnp.zeros((128, D), F32)
 
-    scoped('prepare', loop)(8, prepare)
+    with jax.named_scope("norm"):
+        for j in range(4):
+            hc[j].wait()
+            if j == 1:
+                for cp in weights(0, 0):
+                    cp.start()
+                gc.start()
+            loop(2 * j + 2, norm, 2 * j)
+    gc.wait()
     enter()
 
     def progress(t):
@@ -306,8 +406,11 @@
 
             @pl.when((c >= 0) & (c < 8))
             def _(st=st, c=c):
-                rs.w_finish(W_ORDERS[0], st, 2 * c, None)
-                rs.w_finish(W_ORDERS[1], st, 2 * c + 1, None)
+                rs.w_wait(st, 2 * c, 2, c)
+                rs.w_finish(W_ORDERS[0], st, 2 * c, c, None)
+                rs.w_finish(W_ORDERS[1], st, 2 * c + 1, c, None)
+                if st < 2:
+                    rs.o_wait(st, c)
                 rs.o_finish(0, st, c)
                 rs.o_finish(1, st, c)
 
@@ -319,11 +422,10 @@
             for cp in weights(c + 1, 1 - slot):
                 cp.start()
 
-        for cp in weights(c, slot):
-            cp.wait()
+        weights_here(slot)
         win, wout = s.WA.at[slot, :, pl.ds(0, 512)], s.WB.at[at_multiple(512 * slot, 512)]
         places = units_at(c)
-        bias = jnp.concatenate([s.b_in[:, at_multiple(at, 128)] for at in places], axis=1)
+        bias = jnp.concatenate([s.b_first[:, at_multiple(at, 128)] for at in places], axis=1)
         bacc = jnp.zeros((8, 512), F32)
         for rt in range(2):
             rows = pl.ds(512 * rt, 512)
@@ -349,8 +451,8 @@
             tile = t_dot(nb[:, pl.ds(256 * q, 256)], dpre[...]).astype(BF)
             for i in range(2):
                 s.GW[2 * c + i, q // 2, q % 2] = tile[:, 256 * i : 256 * i + 256].reshape(2, 2, 64, 256)
-        rs.w_copy(W_ORDERS[0], 0, 2 * c).start()
-        rs.w_copy(W_ORDERS[1], 0, 2 * c + 1).start()
+        rs.w_copy(W_ORDERS[0], 0, 2 * c, c).start()
+        rs.w_copy(W_ORDERS[1], 0, 2 * c + 1, c).start()
         for h in range(4):
             part = pl.ds(256 * h, 256)
             out[part, :] += dot(act[part, :], wout[...])
@@ -360,28 +462,23 @@
     loop(8, scoped('chunk', chunk))
     for j in range(4):
         s.VEC[j : j + 1, :] = jnp.sum(s.bcol[:, 1024 * j : 1024 * j + 1024], axis=0, keepdims=True)
-    s.VEC[4:5, :] = jnp.sum(s.bsum[...], axis=0, keepdims=True)
+    s.VEC[4:5, :] = column_sums(s)
     s.VEC[5:8, :] = jnp.zeros((3, D), F32)
 
     def finish_all():
         def units(c):
             places = units_at(c)
-            rs.w_finish(W_ORDERS[0], 3, 2 * c, places[:2])
-            rs.w_finish(W_ORDERS[1], 3, 2 * c + 1, places[2:])
+            rs.w_wait(3, 2 * c, 2, c)
+            rs.w_finish(W_ORDERS[0], 3, 2 * c, c, places[:2])
+            rs.w_finish(W_ORDERS[1], 3, 2 * c + 1, c, places[2:])
             rs.o_finish(0, 3, c)
             rs.o_finish(1, 3, c)
 
         loop(8, units)
 
     def wait_sent():
-        def units(c):
-            for st in range(4):
-                rs.w_copy(W_ORDERS[0], st, 2 * c).wait_send()
-                rs.w_copy(W_ORDERS[1], st, 2 * c + 1).wait_send()
-                rs.o_wait_sent(0, st, c)
-                rs.o_wait_sent(1, st, c)
-
-        loop(8, units)
+        rs.w_wait_sent(16)
+        rs.o_wait_sent()
 
     return progress, finish_all, wait_sent
 
@@ -393,16 +490,17 @@
     def weights(gr, slot):
         return [
             pltpu.make_async_copy(
-                s.w_qkv.at[:, at_multiple(j * 1024 + gr * 256, 256)], s.WA.at[slot, :, pl.ds(256 * j, 256)], s.qsem.at[slot, j]
+                s.w_qkv.at[:, at_multiple(j * 1024 + gr * 256, 256)], s.WA.at[slot, :, pl.ds(256 * j, 256)], s.qsem.at[slot]
             )
             for j in range(3)
         ]
 
-    hc, gc = load_inputs(s)
+    hc, vc, gc = load_inputs(s, s.hb_qkv, s.hb_dense)
     for cp in weights(0, 0):
         cp.start()
     dc = pltpu.make_async_copy(s.w_dense, s.WB, s.lsem.at[1, 0])
     dc.start()
+    gc.start()
     place = lax.broadcasted_iota(jnp.int32, (8, SEQ), 1)
     start = jnp.zeros((8, SEQ), jnp.int32)
     end = jnp.int32(0)
@@ -432,27 +530,25 @@
         qidx = lax.broadcasted_iota(jnp.int32, (256, 256), 1) + 256 * qb
         st = start[0:1, 256 * qb : 256 * qb + 256]
         mask_at(qb, kb)[...] = jnp.where((kidx >= st) & (kidx <= qidx), 0.0, -1e9).astype(BF)
-    for cp in hc:
+    for cp in vc:
         cp.wait()
-    scoped('norm', layer_norm)(staged_rows(s), s.gain[...], s.shift[...], nb)
+
+    def norm(i):
+        at = at_multiple(i * 128, 128)
+        nb[at, :] = layer_norm(staged_rows(s, i), s.gain[...], s.shift[...])
+        dn[at, :] = jnp.zeros((128, D), F32)
+
+    with jax.named_scope("norm"):
+        for j in range(4):
+            hc[j].wait()
+            loop(2 * j + 2, norm, 2 * j)
     gc.wait()
     dc.wait()
-    s.bsum[...] = jnp.zeros((8, D), F32)
-
-    def d_context(i):
-        at = at_multiple(i * 512, 512)
-        for q in range(4):
-            dcT[pl.ds(256 * q, 256), at] = dot_t(s.WB[pl.ds(256 * q, 256), :], g[at, :]).astype(BF)
-        s.bsum[...] += jnp.sum(g[at, :].astype(F32).reshape(64, 8, D), axis=0)
-        dn[at, :] = jnp.zeros((512, D), F32)
-
-    scoped('dctx', loop)(2, d_context)
     enter()
     E = lambda qb, n: s.GO.at[n + 3 * (qb % 2)]
     DS = lambda n: s.GO.at[11 + n]
     kT, vT = s.GO.at[6], s.GO.at[7]
     query, key, value, d_query = (s.RO2.at[n, :, pl.ds(256 * k, 256)] for n in range(2) for k in range(2))
-    ones = jnp.ones((16, SEQ), BF)
     lane = lax.broadcasted_iota(jnp.int32, (256, 256), 1)
 
     def turn(x, i, sign):
@@ -481,9 +577,11 @@
     def finish(gr, st):
         @pl.when(gr >= 0)
         def _():
+            rs.w_wait(st, 3 * gr, 3, gr)
             for j, order in enumerate(QKV_ORDERS):
                 at = 1024 * j + 256 * gr
-                rs.w_finish(order, st, 3 * gr + j, (at, at + 128))
+                rs.w_finish(order, st, 3 * gr + j, gr, (at, at + 128))
+            rs.d_finish(st, gr)
 
     def group(gr):
         slot = lax.rem(gr, 2)
@@ -493,10 +591,9 @@
             for cp in weights(gr + 1, 1 - slot):
                 cp.start()
 
-        for cp in weights(gr, slot):
-            cp.wait()
+        pltpu.make_async_copy(s.w_qkv.at[:, pl.ds(0, 768)], s.WA.at[slot], s.qsem.at[slot]).wait()
         w = s.WA.at[slot]
-        bq = jnp.concatenate([s.b_qkv[:, at_multiple(1024 * j + gr * 256, 256)] for j in range(3)], axis=1)
+        bq = jnp.concatenate([s.b_first[:, at_multiple(1024 * j + gr * 256, 256)] for j in range(3)], axis=1)
 
         with jax.named_scope("project"):
             for i in range(4):
@@ -509,39 +606,53 @@
                 value[at, :] = raw[:, 512:768].astype(BF)
                 vT[:, at] = raw[:, 512:768].T.astype(BF)
         crow = at_multiple(gr * 256, 256)
+        for i in range(2):
+            at = pl.ds(512 * i, 512)
+            dcT[crow, at] = dot_t(s.WB[crow, :], g[at, :]).astype(BF)
         s.PD[...] = jnp.zeros((SEQ, 512), F32)
 
         def keys_of(qb):
             return list(range(max(0, qb - 2), qb + 1))
 
-        def score(qb, n, kb, q4):
-            b = mask_at(qb, kb)[...].astype(F32)
-            sc = dot_t(key[pl.ds(256 * kb, 256), :], q4) + jnp.concatenate([b] * 4, axis=1)
-            S1[pl.ds(256 * n, 256), :] = sc
-            return jnp.max(sc, axis=0, keepdims=True)
+        def score(qb, q4):
+            kbs = keys_of(qb)
+            m = None
+            for n, kb in enumerate(kbs):
+                b = mask_at(qb, kb)[...].astype(F32)
+                part = dot_t(key[pl.ds(256 * kb, 256), :], q4) + jnp.concatenate([b] * 4, axis=1)
+                S1[pl.ds(256 * n, 256), :] = part
+                top = jnp.max(part, axis=0, keepdims=True)
+                m = top if m is None else jnp.maximum(m, top)
+            return m
 
         def weigh(qb, n, m):
-            E(qb, n)[...] = jnp.exp(S1[pl.ds(256 * n, 256), :] - m).astype(BF)
-
-        def context(qb):
+            e = jnp.exp(S1[pl.ds(256 * n, 256), :] - m)
+            E(qb, n)[...] = e.astype(BF)
+            return jnp.sum(e, axis=0, keepdims=True)
+
+        def context(qb, total):
             kbs = keys_of(qb)
             nk = len(kbs)
             win, qs = pl.ds(256 * kbs[0], 256 * nk), pl.ds(256 * qb, 256)
             ev = s.GO[3 * (qb % 2) : 3 * (qb % 2) + nk].reshape(256 * nk, D)
-            cx = dot(jnp.concatenate([vT[:, win], ones[:, 0 : 256 * nk]], axis=0), ev)
-            li = 1.0 / cx[256:257, :]
+            cx = dot(vT[:, win], ev)
+            li = 1.0 / total
             lsel = rows4(li)
             cT = diag(cx) * lsel
             dcs = (dcT[crow, qs].astype(F32) * lsel).astype(BF).astype(F32)
             dcT[crow, qs] = cT.astype(BF)
             return sum4(cT * dcs), stack(dcs.T.astype(BF))
 
-        def back(qb, n, kb, q4, inner, dst):
-            ks = pl.ds(256 * kb, 256)
-            dP = dot_t(value[ks, :], dst)
-            DS(n)[...] = (E(qb, n)[...].astype(F32) * (dP - inner)).astype(BF)
-            s.PD[ks, 256:512] += dot(E(qb, n)[...], dst)
-            s.PD[ks, 0:256] += dot(DS(n)[...], q4)
+        def back(qb, q4, inner, dst):
+            kbs = keys_of(qb)
+            nk = len(kbs)
+            win = pl.ds(256 * kbs[0], 256 * nk)
+            ev = s.GO[3 * (qb % 2) : 3 * (qb % 2) + nk].reshape(256 * nk, D)
+            s.PD[win, 256:512] += dot(ev, dst)
+            for n, kb in enumerate(kbs):
+                dP = dot_t(value[pl.ds(256 * kb, 256), :], dst)
+                DS(n)[...] = (E(qb, n)[...].astype(F32) * (dP - inner)).astype(BF)
+            s.PD[win, 0:256] += dot(s.GO[11 : 11 + nk].reshape(256 * nk, D), q4)
 
         def back_queries(qb):
             kbs = keys_of(qb)
@@ -551,24 +662,18 @@
 
         with jax.named_scope("heads"):
             q4 = stack(query[0:256, :])
-            m = score(0, 0, 0, q4)
-            weigh(0, 0, m)
-            inner, dst = context(0)
+            inner, dst = context(0, weigh(0, 0, score(0, q4)))
             for qb in range(4):
-                kbs, after = keys_of(qb), keys_of(qb + 1) if qb < 3 else []
-                q4_after = stack(query[256 * qb + 256 : 256 * qb + 512, :]) if after else None
-                m = None
-                for n in range(max(len(kbs), len(after))):
-                    if n < len(after):
-                        top = score(qb + 1, n, after[n], q4_after)
-                        m = top if m is None else jnp.maximum(m, top)
-                    if n < len(kbs):
-                        back(qb, n, kbs[n], q4, inner, dst)
-                for n in range(len(after)):
-                    weigh(qb + 1, n, m)
+                q4_after = None
+                if qb < 3:
+                    q4_after = stack(query[256 * qb + 256 : 256 * qb + 512, :])
+                    m = score(qb + 1, q4_after)
+                back(qb, q4, inner, dst)
+                if qb < 3:
+                    total = sum(weigh(qb + 1, n, m) for n in range(len(keys_of(qb + 1))))
                 back_queries(qb)
-                if after:
-                    inner, dst = context(qb + 1)
+                if qb < 3:
+                    inner, dst = context(qb + 1, total)
                 q4 = q4_after
         scoped('reduce', finish)(gr - 2, 1)
         for i in range(4):
@@ -580,7 +685,11 @@
             for j in range(3):
                 s.GW[3 * gr + j, q // 2, q % 2] = tile[:, 256 * j : 256 * j + 256].reshape(2, 2, 64, 256)
         for j, order in enumerate(QKV_ORDERS):
-            rs.w_copy(order, 0, 3 * gr + j).start()
+            rs.w_copy(order, 0, 3 * gr + j, gr).start()
+        tile = dot(dcT[crow, :], g[...]).astype(BF)
+        for j in range(4):
+            s.GW[12 + gr, j // 2, j % 2] = tile[:, 256 * j : 256 * j + 256].reshape(2, 2, 64, 256)
+        rs.d_start(0, gr)
         for j in range(3):
             s.bcol[:, at_multiple(1024 * j + gr * 256, 256)] = jnp.sum(
                 (d_query[...] if j == 0 else s.RO3[:, 256 * j - 256 : 256 * j]).astype(F32).reshape(128, 8, 256), axis=0
@@ -595,19 +704,12 @@
 
     loop(4, scoped('group', group))
 
-    for q in range(4):
-        tile = dot(dcT[pl.ds(256 * q, 256), :], g[...]).astype(BF)
-        for j in range(4):
-            s.GW[12 + j, q // 2, q % 2] = tile[:, 256 * j : 256 * j + 256].reshape(2, 2, 64, 256)
-    for j in range(4):
-        rs.w_copy(DENSE_ORDERS[j], 0, 12 + j).start()
-
     for i in range(4):
         at = pl.ds(256 * i, 256)
         S1[at, :] = t_dot(dcT[:, at], s.WB[...])
     for j in range(3):
         s.VEC[j : j + 1, :] = jnp.sum(s.bcol[:, 1024 * j : 1024 * j + 1024], axis=0, keepdims=True)
-    s.VEC[3:4, :] = jnp.sum(s.bsum[...], axis=0, keepdims=True)
+    s.VEC[3:4, :] = column_sums(s)
     s.VEC[6:8, :] = jnp.zeros((2, D), F32)
 
     def progress(t):
@@ -617,27 +719,16 @@
             finish(2, 2)
         if 8 <= t < 11:
             finish(3, t - 8)
-            for j in range(4):
-                rs.w_finish(DENSE_ORDERS[j], t - 8, 12 + j, None)
 
     def finish_all():
         def units(gr):
             finish(gr, 3)
 
         loop(4, units)
-        for j in range(4):
-            rs.w_finish(DENSE_ORDERS[j], 3, 12 + j, (3072 + 256 * j, 3200 + 256 * j))
 
     def wait_sent():
-        def units(gr):
-            for st in range(4):
-                for j, order in enumerate(QKV_ORDERS):
-                    rs.w_copy(order, st, 3 * gr + j).wait_send()
-
-        loop(4, units)
-        for j in range(4):
-            for st in range(4):
-                rs.w_copy(DENSE_ORDERS[j], st, 12 + j).wait_send()
+        rs.w_wait_sent(12)
+        rs.d_wait_sent()
 
     return progress, finish_all, wait_sent
 
@@ -661,7 +752,7 @@
     def to_other(src, dst, ss, sr):
         return pltpu.make_async_remote_copy(src_ref=src, dst_ref=dst, send_sem=ss, recv_sem=sr, device_id=other, device_id_type=MESH)
 
-    def role(is_attention, run, bias):
+    def role(is_attention, run):
         progress, finish_all, wait_sent = run(s, rs, enter)
         own_half = 0 if is_attention else 1
         mine, theirs = pl.ds(512 * own_half, 512), pl.ds(512 * (1 - own_half), 512)
@@ -673,7 +764,7 @@
 
         def pack(i):
             at = at_multiple(i * 128, 128)
-            branch[at, :] = (s.ACC[1, at, :] + bias[...]).astype(BF)
+            branch[at, :] = (s.ACC[1, at, :] + s.b_last[...]).astype(BF)
             s.WB[at, :] = s.ACC[0, at, :].astype(BF)
 
         scoped('pack', loop)(8, pack)
@@ -686,7 +777,8 @@
             branch.at[pl.ds(512 * (1 - own_half) + 128 * (n // 2), 128), pl.ds(512 * (n % 2), 512)] for n in range(8)
         )
         give, land = (give_feed, to_feed) if is_attention else (give_attention, to_attention)
-        moves = [to_other(src, dst, s.xs.at[n], s.xr.at[n]) for n, (src, dst) in enumerate(zip(give, land))]
+        moves = [to_other(src, dst, s.xs.at[0], s.xr.at[0]) for src, dst in zip(give, land)]
+        all_moves = to_other(s.WA, s.WA, s.xs.at[0], s.xr.at[0])
         for cp in moves:
             cp.start()
         def start_vectors(hop):
@@ -706,20 +798,13 @@
                 scoped('vec', cp.wait)()
             s.VEC[...] += s.VRECV[3 * hop] + s.VRECV[3 * hop + 1] + s.VRECV[3 * hop + 2]
 
-        if not is_attention:
+        if is_attention:
+            scoped('reduce7', progress)(7)
+        else:
             copies = start_vectors(0)
-            for t in range(8, 8 + LAGS[2]):
-                scoped(f'reduce{t}', progress)(t)
-                if t == 9:
-                    end_vectors(0, copies)
-                    copies = start_vectors(1)
-            end_vectors(1, copies)
-        else:
-            progress(7)
+        scoped('reduce8', progress)(8)
         hc.wait()
-        give, land = (give_attention, to_attention) if is_attention else (give_feed, to_feed)
-        for n, (src, dst) in enumerate(zip(give, land)):
-            scoped('moves', to_other(src, dst, s.xs.at[n], s.xr.at[n]).wait_recv)()
+        scoped('moves', all_moves.wait_recv)()
         s.lnsum[...] = jnp.zeros((2, 8, D), F32)
 
         def last(i):
@@ -766,15 +851,20 @@
             for j in range(2):
                 s.VEC[4 + j : 5 + j, :] = jnp.sum(s.lnsum[j], axis=0, keepdims=True)
         if is_attention:
-            for hop in range(2):
-                copies = start_vectors(hop)
-                scoped(f'reduce{8 + hop}', progress)(8 + hop)
-                end_vectors(hop, copies)
+            copies = start_vectors(0)
+            scoped('reduce9', progress)(9)
+            end_vectors(0, copies)
+            copies = start_vectors(1)
+            scoped('reduce10', progress)(10)
+        else:
+            end_vectors(0, copies)
+            copies = start_vectors(1)
+            for t in range(9, 8 + LAGS[2]):
+                scoped(f'reduce{t}', progress)(t)
+        scoped('finish', finish_all)()
+        end_vectors(1, copies)
         vx = to_other(s.VEC, s.VPART, s.vs.at[6], s.vr.at[6])
         vx.start()
-        if is_attention:
-            scoped('reduce10', progress)(10)
-        scoped('finish', finish_all)()
 
         def split(first, size, half):
             return pl.ds(first, size) if extra > 1 else pl.ds(first + half * (size // 2), size // 2)
@@ -796,11 +886,12 @@
             cp.start()
             local.append(cp)
         vx.wait()
-        s.o_vec[0 if is_attention else 1] = s.VEC[...]
-        s.o_vec[1 if is_attention else 0] = s.VPART[...]
+        for n, (src, k) in enumerate(((s.VEC, own_half), (s.VPART, 1 - own_half))):
+            cp = pltpu.make_async_copy(src, s.o_vec.at[k], s.fl.at[7 + n])
+            cp.start()
+            local.append(cp)
         scoped('sent', wait_sent)()
-        for cp in moves:
-            cp.wait_send()
+        all_moves.wait_send()
         for cp in outs + local:
             cp.wait()
         for cp in sent:
@@ -808,22 +899,22 @@
         for n, (src, dst) in enumerate(pieces(not is_attention, own_half)):
             to_other(src, dst, s.fs.at[n], s.fr.at[n]).wait_recv()
 
-    pl.when(pr == 0)(lambda: role(True, attention_role, s.b_dense))
-    pl.when(pr == 1)(lambda: role(False, feed_role, s.b_out))
+    pl.when(pr == 0)(lambda: role(True, attention_role))
+    pl.when(pr == 1)(lambda: role(False, feed_role))
 
 
 def call(extra, *args):
     rows = 32 if extra == 1 else 64
     outw = 128 if extra == 1 else 256
-    anywhere, vmem, smem = (pl.BlockSpec(memory_space=m) for m in (pl.ANY, pltpu.VMEM, pltpu.SMEM))
+    anywhere, smem = (pl.BlockSpec(memory_space=m) for m in (pl.ANY, pltpu.SMEM))
     shapes = [
         ((512, D), BF), ((SEQ, D), BF), ((rows, 3072), F32), ((rows, D), F32), ((rows, FF), F32), ((outw, D), F32), ((2, 8, D), F32),
     ]
     return pl.pallas_call(
         partial(kernel, extra),
         out_shape=[jax.ShapeDtypeStruct(*x) for x in shapes],
-        in_specs=[anywhere, smem, vmem, vmem, anywhere, vmem, anywhere, vmem, anywhere, vmem, anywhere, vmem, anywhere],
-        out_specs=[anywhere] * 6 + [vmem],
+        in_specs=[anywhere, smem] + [anywhere] * 11,
+        out_specs=[anywhere] * 7,
         scratch_shapes=[pltpu.VMEM(shape, kind) for _, shape, kind in SCRATCH]
         + [pltpu.SemaphoreType.DMA(shape) for _, shape in SEMS]
         + [pltpu.SemaphoreType.REGULAR],

time: 132 us -> 130 us (0.985)
  Pallas kernels: 131 us -> 129 us
    pallas_call x1, Pallas kernels: 126 us -> 124 us  [call(): pl.pallas_call(partial(kernel, extra), out_shape=[jax.ShapeDtypeStruct(*x...]
where the time goes in v3:
time: 130 us
  Pallas kernels  129 us (99%)
    pallas_call x1, Pallas kernels, call(): pl.pallas_call(partial(kernel, extra), out_shape=[jax.ShapeDtypeStruct(*x...  124 us
    pallas_call x1, Pallas kernels, body(): pl.pallas_call(partial(deliver, count), out_shape=[jax.ShapeDtypeStruct(x...  5.26 us

profile of v3, /device:TPU:3, one launch (start us, length us, event | category | flops | bytes accessed | tf_op | source)
XLA Modules:
  0.0 129.9 jit_solution(2068514196339169785)
XLA Ops:
  0.6 123.8 %shard_map.220 = (bf16[512,1024]{1,0:T(8,128)(2,1)}, bf16[1024,1024]{1,0:T(8,128)(2,1)}, f32[32,3072]{1,0:T(8,128)}, f32[32,1024]{1,0:T(8,128)}, f32[32,4096]{1,...) custom-call(bf16[1024,1024]{1,0:T(8,128)(2,1)} %refs_0_.1, s32[1,8]{1,0:T(1,128)} %refs_1_.1, f32[1,1024]{1,0:T(1,128)} %bitcast.14, ...), custom_call_target="tpu_custom_call" | custom-call | flops 49999998976 | bytes 40000000 | tf_op jit(solution)/shard_map/pallas_call | solution.py:913
  124.4 5.3 %shard_map.221 = (bf16[512,1024]{1,0:T(8,128)(2,1)}, bf16[1024,1024]{1,0:T(8,128)(2,1)}, f32[32,3072]{1,0:T(8,128)}, f32[32,1024]{1,0:T(8,128)}, f32[32,4096]{1,...) custom-call(bf16[512,1024]{1,0:T(8,128)(2,1)} %get-tuple-element.31., ...), custom_call_target="tpu_custom_call" | custom-call | tf_op jit(solution)/shard_map/pallas_call | solution.py:990

commit v4 on v3

--- a/solution.py
+++ b/solution.py
@@ -417,7 +417,7 @@
     def chunk(c):
         slot = lax.rem(c, 2)
 
-        @pl.when(c < 7)
+        @pl.when((c < 7) & (c != 1))
         def _():
             for cp in weights(c + 1, 1 - slot):
                 cp.start()
@@ -453,10 +453,35 @@
                 s.GW[2 * c + i, q // 2, q % 2] = tile[:, 256 * i : 256 * i + 256].reshape(2, 2, 64, 256)
         rs.w_copy(W_ORDERS[0], 0, 2 * c, c).start()
         rs.w_copy(W_ORDERS[1], 0, 2 * c + 1, c).start()
-        for h in range(4):
-            part = pl.ds(256 * h, 256)
-            out[part, :] += dot(act[part, :], wout[...])
-            dn[part, :] += dot_t(dpre[part, :], win[...])
+
+        @pl.when(c == 0)
+        def _():
+            def keep(i):
+                at = at_multiple(256 * i, 256)
+                for k in range(4):
+                    s.GW[8 + k, i // 2, i % 2] = s.A[2, at, 256 * k : 256 * k + 256].reshape(2, 2, 64, 256)
+
+            loop(4, keep)
+
+        @pl.when(c == 1)
+        def _():
+            def kept(h):
+                part = at_multiple(256 * h, 256)
+                for i in range(2):
+                    out[part, :] += dot(s.GW[8 + i, h // 2, h % 2].reshape(256, 256), s.WB[256 * i : 256 * i + 256, :])
+                    dn[part, :] += dot_t(s.GW[10 + i, h // 2, h % 2].reshape(256, 256), s.WA[0, :, 256 * i : 256 * i + 256])
+
+            loop(4, kept)
+            for cp in weights(2, 0):
+                cp.start()
+
+        @pl.when(c > 0)
+        def _():
+            for h in range(4):
+                part = pl.ds(256 * h, 256)
+                out[part, :] += dot(act[part, :], wout[...])
+                dn[part, :] += dot_t(dpre[part, :], win[...])
+
         scoped('reduce', progress)(c)
 
     loop(8, scoped('chunk', chunk))

time: 130 us -> 130 us (level)
  no operation moved by 1% of the time
where the time goes in v4:
time: 130 us; the launch traced here: 129 us
  Pallas kernels  128 us (98%)
    pallas_call x1, Pallas kernels, call(): pl.pallas_call(partial(kernel, extra), out_shape=[jax.ShapeDtypeStruct(*x...  123 us
    pallas_call x1, Pallas kernels, body(): pl.pallas_call(partial(deliver, count), out_shape=[jax.ShapeDtypeStruct(x...  5.26 us

profile of v4, /device:TPU:3, one launch (start us, length us, event | category | flops | bytes accessed | tf_op | source)
XLA Modules:
  0.0 128.9 jit_solution(8670878073125344268)
XLA Ops:
  0.6 122.8 %shard_map.220 = (bf16[512,1024]{1,0:T(8,128)(2,1)}, bf16[1024,1024]{1,0:T(8,128)(2,1)}, f32[32,3072]{1,0:T(8,128)}, f32[32,1024]{1,0:T(8,128)}, f32[32,4096]{1,...) custom-call(bf16[1024,1024]{1,0:T(8,128)(2,1)} %refs_0_.1, s32[1,8]{1,0:T(1,128)} %refs_1_.1, f32[1,1024]{1,0:T(1,128)} %bitcast.14, ...), custom_call_target="tpu_custom_call" | custom-call | flops 49999998976 | bytes 40000000 | tf_op jit(solution)/shard_map/pallas_call | solution.py:938
  123.4 5.3 %shard_map.221 = (bf16[512,1024]{1,0:T(8,128)(2,1)}, bf16[1024,1024]{1,0:T(8,128)(2,1)}, f32[32,3072]{1,0:T(8,128)}, f32[32,1024]{1,0:T(8,128)}, f32[32,4096]{1,...) custom-call(bf16[512,1024]{1,0:T(8,128)(2,1)} %get-tuple-element.31., ...), custom_call_target="tpu_custom_call" | custom-call | tf_op jit(solution)/shard_map/pallas_call | solution.py:1015

commit v5 on v4

--- a/solution.py
+++ b/solution.py
@@ -878,9 +878,9 @@
         if is_attention:
             copies = start_vectors(0)
             scoped('reduce9', progress)(9)
+            scoped('reduce10', progress)(10)
             end_vectors(0, copies)
             copies = start_vectors(1)
-            scoped('reduce10', progress)(10)
         else:
             end_vectors(0, copies)
             copies = start_vectors(1)

time: 130 us -> 130 us (level)
  no operation moved by 1% of the time
where the time goes in v5:
time: 130 us; the launch traced here: 129 us
  Pallas kernels  128 us (98%)
    pallas_call x1, Pallas kernels, call(): pl.pallas_call(partial(kernel, extra), out_shape=[jax.ShapeDtypeStruct(*x...  123 us
    pallas_call x1, Pallas kernels, body(): pl.pallas_call(partial(deliver, count), out_shape=[jax.ShapeDtypeStruct(x...  5.26 us

profile of v5, /device:TPU:3, one launch (start us, length us, event | category | flops | bytes accessed | tf_op | source)
XLA Modules:
  0.0 128.9 jit_solution(13786882837491540548)
XLA Ops:
  0.6 122.8 %shard_map.220 = (bf16[512,1024]{1,0:T(8,128)(2,1)}, bf16[1024,1024]{1,0:T(8,128)(2,1)}, f32[32,3072]{1,0:T(8,128)}, f32[32,1024]{1,0:T(8,128)}, f32[32,4096]{1,...) custom-call(bf16[1024,1024]{1,0:T(8,128)(2,1)} %refs_0_.1, s32[1,8]{1,0:T(1,128)} %refs_1_.1, f32[1,1024]{1,0:T(1,128)} %bitcast.14, ...), custom_call_target="tpu_custom_call" | custom-call | flops 49999998976 | bytes 40000000 | tf_op jit(solution)/shard_map/pallas_call | solution.py:938
  123.4 5.3 %shard_map.221 = (bf16[512,1024]{1,0:T(8,128)(2,1)}, bf16[1024,1024]{1,0:T(8,128)(2,1)}, f32[32,3072]{1,0:T(8,128)}, f32[32,1024]{1,0:T(8,128)}, f32[32,4096]{1,...) custom-call(bf16[512,1024]{1,0:T(8,128)(2,1)} %get-tuple-element.31., ...), custom_call_target="tpu_custom_call" | custom-call | tf_op jit(solution)/shard_map/pallas_call | solution.py:1015
